TPU v7x, 256 devices: a whole 4x4x8 slice. The times are simulated.
256 devices in a mesh: ctx: 32 (over z_hi, y, core), dp: 8 (over x, z_lo).
Axes of the slice: x: 4, y: 4, z: 8 (z_hi: 4, z_lo: 2; z = z_hi * 2 + z_lo), core: 2. Of those that a mesh axis runs over, the one named last changes fastest.
Arguments:
- query_rows: bfloat16 [49152, 1536], P(('dp', 'ctx')), parts along dimension 0, may hold values from -5 to 5
- key_rows: bfloat16 [49152, 512], P(('dp', 'ctx')), parts along dimension 0, may hold values from -5 to 5
- value_rows: bfloat16 [49152, 512], P(('dp', 'ctx')), parts along dimension 0, may hold values from -6 to 6
- out_grad: bfloat16 [49152, 1536], P(('dp', 'ctx')), parts along dimension 0, may hold values from -6 to 6
- token_span: int32 [49152], P('dp'), parts along dimension 0, may hold values from 0 to 15, never falling along the last dimension, each value on 1 to 768 neighbouring positions
- visible: int32 [128, 16], P('dp'), parts along dimension 0, may hold values from 0 to 1, as said below
Outputs:
- grad_query: bfloat16 [49152, 1536], P(('dp', 'ctx')), parts along dimension 0
- grad_key: bfloat16 [49152, 512], P(('dp', 'ctx')), parts along dimension 0
- grad_value: bfloat16 [49152, 512], P(('dp', 'ctx')), parts along dimension 0
There are 8 independent parts, one for each index of `dp`. A program takes and returns all parts, laid end to end along the dimension named above; each array names one. Nothing has to cross between parts.
Inputs may be any that keep to these rules, and one draw needn't show every extreme that they name: visible[i][i] is 1 and visible[i][j] is 0 for j > i.
All inputs are finite; a program needn't handle non-finite values.
Results may differ from a plain program's by a relative error of at most 0.018.
Values may be sent and summed in bfloat16 or wider, within the bound.
No kernel may reach another device: no remote copies, remote signals or barrier semaphores. Data moves between devices by JAX's collectives and lax.ppermute only.
A program may use at most 128 MiB of HBM per device.

v0:
```python
import math

import jax
import jax.numpy as jnp
from jax import lax
from jax.sharding import PartitionSpec as P

HEADS = 12
KV_HEADS = 4
HEAD = 128


def span_table(visible, row_spans, col_spans):
    span_ids = jnp.arange(visible.shape[0], dtype=jnp.int32)
    row_hot = (row_spans[:, None] == span_ids[None, :]).astype(jnp.float32)
    col_hot = (col_spans[:, None] == span_ids[None, :]).astype(jnp.float32)
    return jnp.dot(jnp.dot(row_hot, visible.astype(jnp.float32)), col_hot.T)


def per_device(query_rows, key_rows, value_rows, out_grad, token_span, visible):
    own_rows = query_rows.shape[0]
    total_rows = token_span.shape[0]
    group_size = HEADS // KV_HEADS
    scaling = HEAD ** (-0.5)
    kv_width = KV_HEADS * HEAD
    first_own = lax.axis_index("ctx") * own_rows
    own_span = lax.dynamic_slice_in_dim(token_span, first_own, own_rows, 0)
    allowed_all = span_table(visible, own_span, token_span)
    query_heads = query_rows.reshape(own_rows, KV_HEADS, group_size, HEAD)
    grad_heads = out_grad.reshape(own_rows, KV_HEADS, group_size, HEAD)
    keys_all, values_all = (
        lax.all_gather(key_rows, "ctx", axis=0, tiled=True),
        lax.all_gather(value_rows, "ctx", axis=0, tiled=True),
    )
    block_rows = math.gcd(512, total_rows)
    block_count = total_rows // block_rows

    def key_block(first_row, size):
        key_block_rows = lax.dynamic_slice_in_dim(keys_all, first_row, size, 0).reshape(
            size, KV_HEADS, HEAD
        )
        value_block_rows = lax.dynamic_slice_in_dim(values_all, first_row, size, 0).reshape(
            size, KV_HEADS, HEAD
        )
        block_mask = lax.dynamic_slice_in_dim(allowed_all, first_row, size, 1)
        return (key_block_rows, value_block_rows, block_mask)

    def block_scores(key_block_rows, block_mask):
        raw_scores = (
            jnp.einsum(
                "qcgd,kcd->cgqk", query_heads, key_block_rows, preferred_element_type=jnp.float32
            )
            * scaling
        )
        return (raw_scores, block_mask[None, None] > 0)

    def stats_step(block_index, state):
        key_block_rows, value_block_rows, block_mask = key_block(
            block_index * block_rows, block_rows
        )

        def stats_visit(inner):
            raw_scores, seen_mask = block_scores(key_block_rows, block_mask)
            block_top = jnp.max(jnp.where(seen_mask, raw_scores, -1e30), axis=-1)
            new_top = jnp.maximum(inner[0], block_top)
            added = jnp.sum(
                jnp.where(seen_mask, jnp.exp(raw_scores - new_top[..., None]), 0.0), axis=-1
            )
            return (new_top, inner[1] * jnp.exp(inner[0] - new_top) + added)

        return lax.cond(jnp.any(block_mask > 0), stats_visit, lambda inner: inner, state)

    stat_shape = (KV_HEADS, group_size, own_rows)
    row_top, row_total = lax.fori_loop(
        0,
        block_count,
        stats_step,
        (jnp.full(stat_shape, -1e30, jnp.float32), jnp.zeros(stat_shape, jnp.float32)),
    )
    log_total = row_top + jnp.log(row_total)

    def block_probs(key_block_rows, block_mask):
        raw_scores, seen_mask = block_scores(key_block_rows, block_mask)
        probs_full = jnp.where(seen_mask, jnp.exp(raw_scores - log_total[..., None]), 0.0)
        return (probs_full, probs_full.astype(jnp.bfloat16))

    def output_step(block_index, output):
        key_block_rows, value_block_rows, block_mask = key_block(
            block_index * block_rows, block_rows
        )

        def output_visit(inner):
            probs_full, probs_low = block_probs(key_block_rows, block_mask)
            return inner + jnp.einsum(
                "cgqk,kcd->qcgd", probs_low, value_block_rows, preferred_element_type=jnp.float32
            )

        return lax.cond(jnp.any(block_mask > 0), output_visit, lambda inner: inner, output)

    output = lax.fori_loop(
        0, block_count, output_step, jnp.zeros((own_rows, KV_HEADS, group_size, HEAD), jnp.float32)
    )
    row_delta = jnp.transpose(jnp.sum(grad_heads.astype(jnp.float32) * output, axis=-1), (1, 2, 0))

    def block_grads(key_block_rows, value_block_rows, block_mask):
        probs_full, probs_low = block_probs(key_block_rows, block_mask)
        dprobs = jnp.einsum(
            "qcgd,kcd->cgqk", grad_heads, value_block_rows, preferred_element_type=jnp.float32
        )
        dscores_low = (probs_full * (dprobs - row_delta[..., None])).astype(jnp.bfloat16)
        return (probs_low, dscores_low)

    def key_grads_of(probs_low, dscores_low, size):
        dk_block = (
            jnp.einsum(
                "cgqk,qcgd->kcd", dscores_low, query_heads, preferred_element_type=jnp.float32
            ).reshape(size, kv_width)
            * scaling
        )
        dv_block = jnp.einsum(
            "cgqk,qcgd->kcd", probs_low, grad_heads, preferred_element_type=jnp.float32
        ).reshape(size, kv_width)
        return (dk_block, dv_block)

    def query_grad_of(dscores_low, key_block_rows):
        return (
            jnp.einsum(
                "cgqk,kcd->qcgd", dscores_low, key_block_rows, preferred_element_type=jnp.float32
            )
            * scaling
        )

    dq_zero = jnp.zeros((own_rows, KV_HEADS, group_size, HEAD), jnp.float32)

    def grad_step(block_index, state):
        first_row = block_index * block_rows
        key_block_rows, value_block_rows, block_mask = key_block(first_row, block_rows)

        def grad_visit(inner):
            probs_low, dscores_low = block_grads(key_block_rows, value_block_rows, block_mask)
            dk_block, dv_block = key_grads_of(probs_low, dscores_low, block_rows)
            new_dq = inner[0] + query_grad_of(dscores_low, key_block_rows)
            new_dk = lax.dynamic_update_slice_in_dim(inner[1], dk_block, first_row, 0)
            new_dv = lax.dynamic_update_slice_in_dim(inner[2], dv_block, first_row, 0)
            return (new_dq, new_dk, new_dv)

        return lax.cond(jnp.any(block_mask > 0), grad_visit, lambda inner: inner, state)

    buffer_zero = jnp.zeros((total_rows, kv_width), jnp.float32)
    dq_sum, dk_buffer, dv_buffer = lax.fori_loop(
        0, block_count, grad_step, (dq_zero, buffer_zero, buffer_zero)
    )
    dk_own, dv_own = (
        lax.psum_scatter(
            dk_buffer.astype(jnp.bfloat16), "ctx", scatter_dimension=0, tiled=True
        ).astype(jnp.float32),
        lax.psum_scatter(
            dv_buffer.astype(jnp.bfloat16), "ctx", scatter_dimension=0, tiled=True
        ).astype(jnp.float32),
    )
    grad_query = dq_sum.reshape(own_rows, HEADS * HEAD).astype(jnp.bfloat16)
    return (grad_query, dk_own.astype(jnp.bfloat16), dv_own.astype(jnp.bfloat16))


def solution(mesh):
    return jax.shard_map(
        per_device,
        mesh=mesh,
        in_specs=(
            P(("dp", "ctx"), None),
            P(("dp", "ctx"), None),
            P(("dp", "ctx"), None),
            P(("dp", "ctx"), None),
            P("dp"),
            P("dp", None),
        ),
        out_specs=(P(("dp", "ctx"), None), P(("dp", "ctx"), None), P(("dp", "ctx"), None)),
        check_vma=False,
    )
```

profile of v0, /device:TPU:2, one launch (start us, length us, event | category | flops | bytes accessed | tf_op | source)
XLA Modules:
  0.0 642.4 jit_solution(9704448085088670502)
XLA Ops:
  12.0 3.2 fusion.40
  15.2 67.3 %all-gather.3.cloned.1.call-done = bf16[6144,512]{1,0:T(8,128)(2,1)} async-done(((bf16[192,512]{1,0:T(8,128)(2,1)}), bf16[6144,512]{1,0:T(8,128)(2,1)}) %all-gather.3.cloned.1.call-update) | async-done | bytes 6291472 | tf_op jit(solution)/shard_map/all_gather | solution.py:32
  82.5 8.7 %copy.78 = bf16[6144,512]{0,1:T(8,128)(2,1)} copy(bf16[6144,512]{1,0:T(8,128)(2,1)} %all-gather.3.cloned.1.call-done) | data formatting | bytes 12582912 | tf_op jit(solution)/shard_map/while | solution.py:150
  91.1 32.8 %while.48 = (s32[]{:T(128)}, f32[4,3,192]{2,1,0:T(4,128)S(1)}, f32[4,3,192]{2,1,0:T(4,128)S(1)}, f32[192,6144]{1,0:T(8,128)}, bf16[6144,512]{0,1:T(8,128)(2,1)},...) while((s32[]{:T(128)}, f32[4,3,192]{2,1,0:T(4,128)S(1)}, ...), condition=%wide.region_6.7_spmd, body=%wide.region_0.6_spmd.sunk | while | flops 310546944 | bytes 13194489 | solution.py:74
  91.2 1.7 compare_reduce_fusion.6
  93.5 3.8 conditional.6
  97.3 1.7 compare_reduce_fusion.6
  99.8 1.7 compare_reduce_fusion.6
  102.2 1.7 compare_reduce_fusion.6
  104.6 1.7 compare_reduce_fusion.6
  107.0 1.8 compare_reduce_fusion.6
  109.5 1.7 compare_reduce_fusion.6
  111.9 1.7 compare_reduce_fusion.6
  114.3 1.7 compare_reduce_fusion.6
  116.7 1.7 compare_reduce_fusion.6
  119.1 1.7 compare_reduce_fusion.6
  121.5 1.7 compare_reduce_fusion.6
  124.0 28.1 %all-gather.5.cloned.1.call-done = bf16[6144,512]{1,0:T(8,128)(2,1)} async-done(((bf16[192,512]{1,0:T(8,128)(2,1)}), bf16[6144,512]{1,0:T(8,128)(2,1)}) %all-gather.5.cloned.1.call-update) | async-done | bytes 6291472 | tf_op jit(solution)/shard_map/all_gather | solution.py:33
  152.0 8.7 %copy.80 = bf16[6144,512]{0,1:T(8,128)(2,1)} copy(bf16[6144,512]{1,0:T(8,128)(2,1)} %all-gather.5.cloned.1.call-done) | data formatting | bytes 12582912 | tf_op jit(solution)/shard_map/while | solution.py:150
  161.9 32.5 %while.49 = (s32[]{:T(128)}, f32[192,4,3,128]{3,0,2,1:T(8,128)}, f32[192,6144]{1,0:T(8,128)}, bf16[6144,512]{0,1:T(8,128)(2,1)}, bf16[192,4,3,128]{3,0,2,1:T(8,1...) while((s32[]{:T(128)}, f32[192,4,3,128]{3,0,2,1:T(8,128)}, ...), condition=%wide.region_11.12_spmd, body=%wide.region_7.11_spmd.sunk | while | flops 609288192 | bytes 7480553 | solution.py:100
  164.1 5.3 conditional.7
  165.5 3.9 fusion.18
  194.4 2.5 fusion.39
  197.2 3.4 broadcast_in_dim.65.clone
  200.6 3.4 broadcast_in_dim.65
  203.9 37.5 %while.50 = (s32[]{:T(128)}, f32[192,4,3,128]{3,0,2,1:T(8,128)S(1)}, bf16[6144,512]{0,1:T(8,128)(2,1)}, bf16[6144,512]{0,1:T(8,128)(2,1)}, f32[192,6144]{1,0:T(8...) while((s32[]{:T(128)}, ...), condition=%wide.region_17.18_spmd, body=%wide.region_13.17_spmd.sunk | while | flops 1523154944 | bytes 34270600 | solution.py:150
  206.3 8.7 %conditional.8 = ((f32[192,4,3,128]{3,0,2,1:T(8,128)S(1)}, bf16[6144,512]{0,1:T(8,128)(2,1)}, bf16[6144,512]{0,1:T(8,128)(2,1)})) conditional(s32[]{:T(128)} %convert_element_type.84, (f32[192,4,3,128]{3,0,2,1:T(8,128)S(1)}, bf16[6144,512]{0,1:T(8,128)(2,1)}, bf16[6144,512]{0,1:T(8,128)(2,1)}) %tuple.145, (f32[192,512]{1,0:T(8,128)S(1)}, ...), branch_computations={%region_15.15_spmd, %region_16.16_spmd} | conditional | flops 1522958336 | bytes 33483852 | solution.py:147
  210.6 1.8 fusion.24
  241.4 8.6 %copy.85 = bf16[6144,512]{1,0:T(8,128)(2,1)} copy(bf16[6144,512]{0,1:T(8,128)(2,1)} %get-tuple-element.649) | data formatting | bytes 12582912 | tf_op jit(solution)/shard_map/while | solution.py:150
  250.1 8.7 %copy.84 = bf16[6144,512]{1,0:T(8,128)(2,1)} copy(bf16[6144,512]{0,1:T(8,128)(2,1)} %get-tuple-element.648) | data formatting | bytes 12582912 | tf_op jit(solution)/shard_map/while | solution.py:150
  260.6 263.0 %reduce-scatter.5.cloned.1.call-done = bf16[192,512]{1,0:T(8,128)(2,1)} async-done(((bf16[6144,512]{1,0:T(8,128)(2,1)}), bf16[192,512]{1,0:T(8,128)(2,1)}) %reduce-scatter.5.cloned.1.call-update) | async-done | bytes 196624 | tf_op jit(solution)/shard_map/reduce_scatter | solution.py:157
  523.7 112.2 %reduce-scatter.3.cloned.1.call-done = bf16[192,512]{1,0:T(8,128)(2,1)} async-done(((bf16[6144,512]{1,0:T(8,128)(2,1)}), bf16[192,512]{1,0:T(8,128)(2,1)}) %reduce-scatter.3.cloned.1.call-update) | async-done | bytes 196624 | tf_op jit(solution)/shard_map/reduce_scatter | solution.py:154
  (100 shorter events, 61.3 us)
Async XLA Ops:
  7.2 4.7 copy-start
  7.2 4.8 copy-start.1
  7.2 75.3 %all-gather.3.cloned.1.call-start = ((), (), s32[]{:S(2)}) async-start(), calls=%async_computation.2 | async-start | bytes 6488064 | tf_op jit(solution)/shard_map/all_gather | solution.py:32
  7.9 144.1 %all-gather.5.cloned.1.call-start = ((), (), s32[]{:S(2)}) async-start(), calls=%async_computation.3 | async-start | bytes 6488064 | tf_op jit(solution)/shard_map/all_gather | solution.py:33
  8.7 515.0 %reduce-scatter.5.cloned.1.call-start = ((), (), s32[]{:S(2)}) async-start(), calls=%async_computation.5 | async-start | bytes 6488064 | tf_op jit(solution)/shard_map/reduce_scatter | solution.py:157
  250.1 385.8 %reduce-scatter.3.cloned.1.call-start = ((), (), s32[]{:S(2)}) async-start(), calls=%async_computation.4 | async-start | bytes 6488064 | tf_op jit(solution)/shard_map/reduce_scatter | solution.py:154
Sparse Core Ops, SparseCore 0:
  10.6 71.8 all-gather.2
  85.0 66.9 all-gather.4
  250.2 273.4 reduce-scatter.4
  528.7 107.1 reduce-scatter.2
where the time goes:
time: 647 us; the launch traced here: 642 us
  waiting for transfers between devices  472 us (73%)
  other arithmetic  66 us (10%)
  local copies, waits for them, and re-layouts  53.5 us (8%)
  loops' own time  23.5 us (4%)
  between operations  13.9 us (2%)
  matrix products  13.5 us (2%)
    reduce_scatter x1, waiting for transfers between devices, per_device(): lax.psum_scatter(dv_buffer.astype(jnp.bfloat16), 'ctx', scatter_dimension...  263 us
    reduce_scatter x1, waiting for transfers between devices, per_device(): lax.psum_scatter(dk_buffer.astype(jnp.bfloat16), 'ctx', scatter_dimension...  112 us
    all_gather x1, waiting for transfers between devices, per_device(): lax.all_gather(key_rows, 'ctx', axis=0, tiled=True)  67.3 us
    while x7, local copies, waits for them, and re-layouts, per_device(): lax.fori_loop(0, block_count, grad_step, (dq_zero, buffer_zero, buffer_ze...  35.2 us
    all_gather x1, waiting for transfers between devices, per_device(): lax.all_gather(value_rows, 'ctx', axis=0, tiled=True)  28.1 us
    reduce_or x12, other arithmetic, stats_step(): jnp.any(block_mask > 0)  20.8 us
    reduce_or x12, other arithmetic, grad_step(): jnp.any(block_mask > 0)  20.7 us
    reduce_or x12, other arithmetic, output_step(): jnp.any(block_mask > 0)  20.2 us
  transfers between devices with their start and end apart: 4, of which 4 were waited for; matrix products, arithmetic and copies ran while one was open for 8% of the time, Pallas kernels for 0%

commit v1 on v0

v1 whole, which is shorter than its diff:
```python
import functools

import jax
import jax.numpy as jnp
import numpy as np
from jax import lax
from jax.experimental import pallas as pl
from jax.experimental.pallas import tpu as pltpu
from jax.sharding import Mesh, PartitionSpec as P

HEADS = 12
KV_HEADS = 4
GROUP = HEADS // KV_HEADS
HEAD = 128
SCALE = HEAD ** -0.5
LOG2E = 1.4426950408889634
NEG = -1e30
Z, Y, C = 4, 4, 2
T = Y * C
BLK = 192
QT = 256
NQ = Z * BLK // QT
PAIR = 2
KT = PAIR * BLK
NK = Z * T // PAIR
F32 = jnp.float32
BF16 = jnp.bfloat16


def dot(a, b):
    return lax.dot_general(a, b, (((1,), (0,)), ((), ())), preferred_element_type=F32)


def dot_tn(a, b):
    return lax.dot_general(a, b, (((0,), (0,)), ((), ())), preferred_element_type=F32)


def fold(x, op):
    return op(x.reshape(x.shape[0] // 8, 8, x.shape[1]), axis=0)


def attn_kernel(flags, qd_ref, kv_ref, hot_ref, bias_ref, dq_ref, dkv_ref,
                acc, sbuf, pbuf, qt, dot_t, qs, dos, stat_m, stat_l, stat_d, dqt):
    r = pl.program_id(0)

    @pl.when(r == 0)
    def _():
        acc[...] = jnp.zeros_like(acc)

    for h in range(GROUP):
        q = qd_ref[:, h * HEAD:(h + 1) * HEAD]
        g = qd_ref[:, (GROUP + h) * HEAD:(GROUP + h + 1) * HEAD]
        qt[h, :HEAD, :] = q.T
        qt[h, HEAD:, :] = bias_ref[0]
        dot_t[h] = g.T
    stat_m[...] = jnp.full_like(stat_m, NEG)
    stat_l[...] = jnp.zeros_like(stat_l)
    stat_d[...] = jnp.zeros_like(stat_d)
    dqt[...] = jnp.zeros_like(dqt)

    def place(n):
        return n // (T // PAIR), (n % (T // PAIR)) * PAIR

    def rows_of(n, lo):
        zq, t = place(n)
        return jnp.concatenate([kv_ref[t + i, zq, :, lo:lo + HEAD] for i in range(PAIR)], axis=0)

    def over_tiles(body):
        def step(n, carry):
            @pl.when(flags[r * NK + n] > 0)
            def _():
                body(n)
            return carry
        lax.fori_loop(0, NK, step, 0)

    def scores(n):
        zq, t = place(n)
        hot = jnp.concatenate([hot_ref[t + i, zq] for i in range(PAIR)], axis=0)
        lhs = jnp.concatenate([rows_of(n, 0), hot], axis=1)
        for h in range(GROUP):
            s = dot(lhs, qt[h])
            sbuf[n, :, h * QT:(h + 1) * QT] = s
            stat_m[h] = jnp.maximum(stat_m[h], fold(s, jnp.max))

    over_tiles(scores)
    tops = [jnp.max(stat_m[h], axis=0, keepdims=True) for h in range(GROUP)]
    for h in range(GROUP):
        stat_m[h] = jnp.broadcast_to(tops[h], (8, QT))

    def weights(n):
        v = rows_of(n, HEAD)
        for h in range(GROUP):
            cols = slice(h * QT, (h + 1) * QT)
            p = jnp.exp2((sbuf[n, :, cols] - stat_m[h, :1]) * (SCALE * LOG2E))
            dp = dot(v, dot_t[h])
            stat_l[h] += fold(p, jnp.sum)
            stat_d[h] += fold(p * dp, jnp.sum)
            pbuf[n, :, cols] = p.astype(BF16)
            sbuf[n, :, cols] = dp

    over_tiles(weights)
    invs = []
    for h in range(GROUP):
        inv = 1.0 / jnp.sum(stat_l[h], axis=0, keepdims=True)
        delta = jnp.sum(stat_d[h], axis=0, keepdims=True) * inv
        stat_d[h] = jnp.broadcast_to(delta, (8, QT))
        col = jnp.broadcast_to(inv, (HEAD, QT)).T
        q = qd_ref[:, h * HEAD:(h + 1) * HEAD].astype(F32)
        g = qd_ref[:, (GROUP + h) * HEAD:(GROUP + h + 1) * HEAD].astype(F32)
        qs[h] = (q * (col * SCALE)).astype(BF16)
        dos[h] = (g * col).astype(BF16)
        invs.append(inv)

    def grads(n):
        zq, t = place(n)
        k = rows_of(n, 0)
        dk = jnp.zeros((KT, HEAD), F32)
        dv = jnp.zeros((KT, HEAD), F32)
        for h in range(GROUP):
            cols = slice(h * QT, (h + 1) * QT)
            p = pbuf[n, :, cols]
            ds = (p.astype(F32) * (sbuf[n, :, cols] - stat_d[h, :1])).astype(BF16)
            dv += dot(p, dos[h])
            dk += dot(ds, qs[h])
            dqt[h] += dot_tn(k, ds)
        for i in range(PAIR):
            acc[t + i, zq, :, :HEAD] += dk[i * BLK:(i + 1) * BLK]
            acc[t + i, zq, :, HEAD:] += dv[i * BLK:(i + 1) * BLK]

    over_tiles(grads)
    for h in range(GROUP):
        dq_ref[:, h * HEAD:(h + 1) * HEAD] = (dqt[h] * (invs[h] * SCALE)).T.astype(BF16)

    @pl.when(r == NQ - 1)
    def _():
        for i in range(T):
            dkv_ref[i] = acc[i].astype(BF16)


def attention(flags, qd, kv, hot, bias):
    whole = lambda *shape: pl.BlockSpec(shape, lambda r, f: (0,) * len(shape))
    return pl.pallas_call(
        attn_kernel,
        grid_spec=pltpu.PrefetchScalarGridSpec(
            num_scalar_prefetch=1,
            grid=(NQ,),
            in_specs=[
                pl.BlockSpec((QT, 2 * GROUP * HEAD), lambda r, f: (r, 0)),
                whole(T, Z, BLK, 2 * HEAD),
                whole(T, Z, BLK, HEAD),
                pl.BlockSpec((1, HEAD, QT), lambda r, f: (r, 0, 0)),
            ],
            out_specs=[
                pl.BlockSpec((QT, GROUP * HEAD), lambda r, f: (r, 0)),
                whole(T, Z, BLK, 2 * HEAD),
            ],
            scratch_shapes=[
                pltpu.VMEM((T, Z, BLK, 2 * HEAD), F32),
                pltpu.VMEM((NK, KT, GROUP * QT), F32),
                pltpu.VMEM((NK, KT, GROUP * QT), BF16),
                pltpu.VMEM((GROUP, 2 * HEAD, QT), BF16),
                pltpu.VMEM((GROUP, HEAD, QT), BF16),
                pltpu.VMEM((GROUP, QT, HEAD), BF16),
                pltpu.VMEM((GROUP, QT, HEAD), BF16),
                pltpu.VMEM((GROUP, 8, QT), F32),
                pltpu.VMEM((GROUP, 8, QT), F32),
                pltpu.VMEM((GROUP, 8, QT), F32),
                pltpu.VMEM((GROUP, HEAD, QT), F32),
            ],
        ),
        out_shape=[
            jax.ShapeDtypeStruct((Z * BLK, GROUP * HEAD), BF16),
            jax.ShapeDtypeStruct((T, Z, BLK, 2 * HEAD), BF16),
        ],
        compiler_params=pltpu.CompilerParams(
            dimension_semantics=("arbitrary",), vmem_limit_bytes=60 * 1024 * 1024
        ),
    )(flags, qd, kv, hot, bias)


def masks(token_span, visible, t_index):
    spans = token_span.reshape(Z, T, BLK)
    ids = jnp.arange(HEAD, dtype=jnp.int32)
    hot = (spans.transpose(1, 0, 2)[..., None] == ids).astype(BF16)
    mine = lax.dynamic_index_in_dim(spans, t_index, 1, keepdims=False).reshape(NQ, QT)
    span_ids = jnp.arange(visible.shape[0], dtype=jnp.int32)
    mine_hot = (mine[..., None] == span_ids).astype(F32)
    seen = jnp.einsum("rqs,sk->rkq", mine_hot, visible.astype(F32))
    bias = jnp.where(seen > 0, 0.0, NEG).astype(BF16)
    bias = jnp.pad(bias, ((0, 0), (0, HEAD - visible.shape[0]), (0, 0)))
    key_has = jnp.any(token_span.reshape(NK, KT)[..., None] == span_ids, axis=1)
    seen_any = jnp.any(seen > 0, axis=2)
    flags = jnp.any(key_has[None] & seen_any[:, None], axis=2).astype(jnp.int32)
    return hot, bias, flags.reshape(-1)


def per_device(query_rows, key_rows, value_rows, out_grad, token_span, visible):
    t_index = lax.axis_index("y") * C + lax.axis_index("core")
    hot, bias, flags = masks(token_span, visible, t_index)

    def by_head(x):
        return x.reshape(BLK, KV_HEADS, -1).transpose(1, 0, 2)

    def swap(x):
        return lax.all_to_all(x, "z", 0, 0, tiled=True)

    kv = swap(jnp.concatenate([by_head(key_rows), by_head(value_rows)], axis=2))
    kv = lax.all_gather(kv, ("y", "core"), axis=0)
    qd = swap(jnp.concatenate([by_head(query_rows), by_head(out_grad)], axis=2))
    dq, dkv = attention(flags, qd.reshape(Z * BLK, -1), kv, hot, bias)
    dkv = lax.psum_scatter(dkv, ("y", "core"), scatter_dimension=0, tiled=False)
    dkv = swap(dkv).transpose(1, 0, 2)
    dq = swap(dq.reshape(Z, BLK, GROUP * HEAD)).transpose(1, 0, 2).reshape(BLK, HEADS * HEAD)
    dk = dkv[..., :HEAD].reshape(BLK, KV_HEADS * HEAD)
    dv = dkv[..., HEAD:].reshape(BLK, KV_HEADS * HEAD)
    return dq, dk, dv


def solution(mesh):
    dp = mesh.shape["dp"]
    split = Mesh(mesh.devices.reshape(Z, Y, C, dp), ("z", "y", "core", "dp"))
    rows = P(("dp", "z", "y", "core"), None)
    return jax.shard_map(
        per_device,
        mesh=split,
        in_specs=(rows, rows, rows, rows, P("dp"), P("dp", None)),
        out_specs=(rows, rows, rows),
        check_vma=False,
    )
```

time: 647 us -> 187 us (0.29)
  waiting for transfers between devices: 472 us -> 59 us
  other arithmetic: 66 us -> 4.16 us
  blocking collectives: 0 us -> 47.8 us
  local copies, waits for them, and re-layouts: 53.5 us -> 7.66 us
  Pallas kernels: 0 us -> 42.7 us
  loops' own time: 23.5 us -> 0 us
  matrix products: 13.5 us -> 0.33 us
  starting transfers between devices: 0.16 us -> 10.6 us
    reduce_scatter x2 -> x1, waiting for transfers between devices: 375 us -> 30.8 us  [per_device(): dkv = lax.psum_scatter(dkv, ('y', 'core'), scatter_dimension=0, tiled=False)]
    all_gather x2 -> x1, waiting for transfers between devices: 95.3 us -> 0.59 us  [per_device(): kv = lax.all_gather(kv, ('y', 'core'), axis=0)]
    reduce_or x36 -> x2, other arithmetic: 61.7 us -> 0.52 us  [the longest x1 0.36 us: masks(): key_has = jnp.any(token_span.reshape(NK, KT)[..., None] == span_ids, axis=1)]
    all_to_all x0 -> x2, blocking collectives: none -> 47.8 us  [swap(): return lax.all_to_all(x, 'z', 0, 0, tiled=True)]
    pallas_call x0 -> x1, Pallas kernels: none -> 42.7 us  [attention(): pl.pallas_call(attn_kernel, grid_spec=pltpu.PrefetchScalarGridSpec(num_sc...]
    while x7 -> x0, local copies, waits for them, and re-layouts: 35.2 us -> none  [per_device(): lax.fori_loop(0, block_count, grad_step, (dq_zero, buffer_zero, buffer_ze...]
    all_to_all x0 -> x2, waiting for transfers between devices: none -> 27.6 us  [swap(): return lax.all_to_all(x, 'z', 0, 0, tiled=True)]
    another operation x39 -> x0, loops' own time: 23.5 us -> none  [the longest x1 8.06 us: per_device(): lax.fori_loop(0, block_count, stats_step, (jnp.full(stat_shape, -1e+30, j...]
  transfers between devices with their start and end apart: 4 -> 4, of which waited for: 4 -> 4; matrix products, arithmetic and copies ran while one was open for 8% -> 4% of each run, Pallas kernels for 0% -> 0%
where the time goes in v1:
time: 187 us; the launch traced here: 186 us
  waiting for transfers between devices  59 us (32%)
  blocking collectives  47.8 us (26%)
  Pallas kernels  42.7 us (23%)
  between operations  14.2 us (8%)
  starting transfers between devices  10.6 us (6%)
  local copies, waits for them, and re-layouts  7.66 us (4%)
  other arithmetic  4.16 us (2%)
    all_to_all x2, blocking collectives, swap(): return lax.all_to_all(x, 'z', 0, 0, tiled=True)  47.8 us
    pallas_call x1, Pallas kernels, attention(): pl.pallas_call(attn_kernel, grid_spec=pltpu.PrefetchScalarGridSpec(num_sc...  42.7 us
    reduce_scatter x1, waiting for transfers between devices, per_device(): dkv = lax.psum_scatter(dkv, ('y', 'core'), scatter_dimension=0, tiled=False)  30.8 us
    all_to_all x2, waiting for transfers between devices, swap(): return lax.all_to_all(x, 'z', 0, 0, tiled=True)  27.6 us
    all_to_all x2, starting transfers between devices, swap(): return lax.all_to_all(x, 'z', 0, 0, tiled=True)  10.5 us
  transfers between devices with their start and end apart: 4, of which 4 were waited for; matrix products, arithmetic and copies ran while one was open for 4% of the time, Pallas kernels for 0%

profile of v1, /device:TPU:2, one launch (start us, length us, event | category | flops | bytes accessed | tf_op | source)
XLA Modules:
  0.0 186.4 jit_solution(16166193238240161173)
XLA Ops:
  7.2 0.0 all-gather.3.cloned.1.call-start
  7.2 1.1 reshape.50
  8.3 1.0 reshape.51
  9.3 0.2 pad_maximum_fusion.1
  9.5 22.2 %all_to_all.20 = bf16[4,192,256]{2,1,0:T(8,128)(2,1)} all-to-all(bf16[4,192,256]{2,1,0:T(8,128)(2,1)S(1)} %copy.50), channel_id=1, replica_groups=mesh['z'=4,'y'=4,'core'=2,'dp'=8] {'z'}, dimensions={0} | all-to-all | bytes 786432 | tf_op jit(solution)/shard_map/all_to_all | solution.py:205
  31.7 0.0 all-gather.3.cloned.1.call-update
  31.8 0.1 bitcast_bitcast_fusion
  31.9 1.1 pad_maximum_fusion
  33.1 3.5 %all-to-all-start = ((bf16[4,192,768]{2,1,0:T(8,128)(2,1)}), bf16[4,192,768]{2,1,0:T(8,128)(2,1)S(1)}, u32[]{:S(2)}, u32[]{:S(2)}) async-start(bf16[4,192,768]{2,1,0:T(8,128)(2,1)} %pad_maximum_fusion), calls=%async_computation | async-start | bytes 2359296 | tf_op jit(solution)/shard_map/all_to_all | solution.py:205
  36.6 0.0 reduce-scatter.2.cloned.1.call-start
  36.7 0.1 reshape.46
  36.8 0.1 eq.47
  36.9 0.4 fusion.2
  37.2 0.3 fusion.6
  37.6 0.2 and_reduce_fusion
  37.7 0.6 reshape.56.flags
  38.4 0.7 pad.4.bias_ref
  39.1 2.3 %fusion.hot_ref = bf16[8,4,192,128]{3,2,1,0:T(8,128)(2,1)} fusion(s32[8,4,192]{2,1,0:T(4,128)S(1)} %copy.51), kind=kLoop, calls=%fused_computation.1 | loop fusion | flops 1572864 | bytes 1597440 | tf_op jit(solution)/shard_map/convert_element_type | solution.py:184
  41.4 17.5 %all-to-all-done = bf16[4,192,768]{2,1,0:T(8,128)(2,1)S(1)} async-done(((bf16[4,192,768]{2,1,0:T(8,128)(2,1)}), bf16[4,192,768]{2,1,0:T(8,128)(2,1)S(1)}, u32[]{:S(2)}, u32[]{:S(2)}) %all-to-all-start) | async-done | bytes 1179680 | tf_op jit(solution)/shard_map/all_to_all | solution.py:205
  58.8 0.6 all-gather.3.cloned.1.call-done
  59.4 0.5 copy-done
  60.0 42.7 %shard_map.85 = (bf16[768,384]{1,0:T(8,128)(2,1)}, bf16[8,4,192,256]{3,2,1,0:T(8,128)(2,1)}) custom-call(s32[48]{0:T(128)} %reshape.56.flags, bf16[768,768]{1,0:T(8,128)(2,1)} %bitcast.38, bf16[8,4,192,256]{3,2,1,0:T(8,128)(2,1)} %bitcast.39, bf16[8,4,192,128]{3,2,1,0:T(8,128)(2,1)} %fusion.hot_ref, bf16[3,128,256]{2,1,0:T(8,128)(2,1)} %pad.4.bias_ref), custom_call_target="tpu_custom_call" | custom-call | tf_op jit(solution)/shard_map/pallas_call | solution.py:142
  102.7 0.0 reduce-scatter.2.cloned.1.call-update
  102.7 1.0 copy-done.1
  103.7 25.6 %all_to_all.21 = bf16[4,192,384]{2,1,0:T(8,128)(2,1)S(1)} all-to-all(bf16[4,192,384]{2,1,0:T(8,128)(2,1)S(1)} %bitcast.45), channel_id=1, replica_groups=mesh['z'=4,'y'=4,'core'=2,'dp'=8] {'z'}, dimensions={0} | all-to-all | bytes 1179648 | tf_op jit(solution)/shard_map/all_to_all | solution.py:205
  129.3 30.8 %reduce-scatter.2.cloned.1.call-done = bf16[1,4,192,256]{3,2,1,0:T(8,128)(2,1)} async-done(((bf16[8,4,192,256]{3,2,1,0:T(8,128)(2,1)}), bf16[1,4,192,256]{3,2,1,0:T(8,128)(2,1)}) %reduce-scatter.2.cloned.1.call-update) | async-done | bytes 393232 | tf_op jit(solution)/shard_map/reduce_scatter | solution.py:211
  160.1 7.0 %all-to-all-start.3 = ((bf16[4,192,256]{2,1,0:T(8,128)(2,1)}), bf16[4,192,256]{2,1,0:T(8,128)(2,1)S(1)}, u32[]{:S(2)}, u32[]{:S(2)}) async-start(bf16[4,192,256]{2,1,0:T(8,128)(2,1)} %bitcast.48), calls=%async_computation.4 | async-start | bytes 786432 | tf_op jit(solution)/shard_map/all_to_all | solution.py:205
  167.1 0.9 copy.59
  168.0 10.1 %all-to-all-done.3 = bf16[4,192,256]{2,1,0:T(8,128)(2,1)S(1)} async-done(((bf16[4,192,256]{2,1,0:T(8,128)(2,1)}), bf16[4,192,256]{2,1,0:T(8,128)(2,1)S(1)}, u32[]{:S(2)}, u32[]{:S(2)}) %all-to-all-start.3) | async-done | bytes 393248 | tf_op jit(solution)/shard_map/all_to_all | solution.py:205
  178.1 0.1 slice_bitcast_fusion
  178.2 0.7 copy.66
  178.9 0.7 copy.67
  (16 shorter events, 0.1 us)
Async XLA Ops:
  7.2 24.6 %copy-start.2 = (bf16[192,1536]{1,0:T(8,128)(2,1)S(1)}, bf16[192,1536]{1,0:T(8,128)(2,1)}, u32[]{:S(2)}) copy-start(bf16[192,1536]{1,0:T(8,128)(2,1)} %param.9) | copy-start | bytes 1769476
  7.2 24.6 %copy-start.3 = (bf16[192,1536]{1,0:T(8,128)(2,1)S(1)}, bf16[192,1536]{1,0:T(8,128)(2,1)}, u32[]{:S(2)}) copy-start(bf16[192,1536]{1,0:T(8,128)(2,1)} %param.6) | copy-start | bytes 1769476
  7.2 52.2 %all-gather.3.cloned.1.call-start = ((), (), s32[]{:S(2)}) async-start(), calls=%async_computation.6 | async-start | bytes 3538944 | tf_op jit(solution)/shard_map/all_gather | solution.py:208
  31.9 4.7 %copy-start.4 = (s32[6144]{0:T(1024)S(1)}, s32[6144]{0:T(1024)}, u32[]{:S(2)}) copy-start(s32[6144]{0:T(1024)} %param.10) | copy-start | bytes 73732
  31.9 5.3 %copy-start.5 = (s32[16,16]{1,0:T(8,128)S(1)}, s32[16,16]{1,0:T(8,128)}, u32[]{:S(2)}) copy-start(s32[16,16]{1,0:T(8,128)} %param.11) | copy-start | bytes 3076
  33.1 25.8 %all-to-all-start = ((bf16[4,192,768]{2,1,0:T(8,128)(2,1)}), bf16[4,192,768]{2,1,0:T(8,128)(2,1)S(1)}, u32[]{:S(2)}, u32[]{:S(2)}) async-start(bf16[4,192,768]{2,1,0:T(8,128)(2,1)} %pad_maximum_fusion), calls=%async_computation | async-start | bytes 2359296 | tf_op jit(solution)/shard_map/all_to_all | solution.py:205
  36.6 123.5 %reduce-scatter.2.cloned.1.call-start = ((), (), s32[]{:S(2)}) async-start(), calls=%async_computation.5 | async-start | bytes 3538944 | tf_op jit(solution)/shard_map/reduce_scatter | solution.py:211
  58.8 1.1 copy-start
  102.7 1.1 copy-start.1
  160.1 18.0 %all-to-all-start.3 = ((bf16[4,192,256]{2,1,0:T(8,128)(2,1)}), bf16[4,192,256]{2,1,0:T(8,128)(2,1)S(1)}, u32[]{:S(2)}, u32[]{:S(2)}) async-start(bf16[4,192,256]{2,1,0:T(8,128)(2,1)} %bitcast.48), calls=%async_computation.4 | async-start | bytes 786432 | tf_op jit(solution)/shard_map/all_to_all | solution.py:205
Sparse Core Ops, SparseCore 0:
  31.9 27.4 all-gather.2
  102.8 57.2 reduce-scatter.1

commit v2 on v1

v2 whole, which is shorter than its diff:
```python
import functools

import jax
import jax.numpy as jnp
import numpy as np
from jax import lax
from jax.experimental import pallas as pl
from jax.experimental.pallas import tpu as pltpu
from jax.sharding import Mesh, PartitionSpec as P

HEADS = 12
KV_HEADS = 4
GROUP = HEADS // KV_HEADS
HEAD = 128
SCALE = HEAD ** -0.5
LOG2E = 1.4426950408889634
NEG = -1e30
LEAST = 2.0 ** -60
MOST = 2.0 ** 60
Z, Y, C = 4, 4, 2
T = Y * C
BLK = 192
QT = 256
NQ = Z * BLK // QT
NB = Z * T
WIDE = 4
NI = NB // WIDE
KT = WIDE * BLK
F32 = jnp.float32
BF16 = jnp.bfloat16


def dot(a, b):
    return lax.dot_general(a, b, (((1,), (0,)), ((), ())), preferred_element_type=F32)


def dot_tn(a, b):
    return lax.dot_general(a, b, (((0,), (0,)), ((), ())), preferred_element_type=F32)


def fold(x, op):
    return op(x.reshape(x.shape[0] // 8, 8, x.shape[1]), axis=0)


def attn_kernel(lists, counts, spot, qd_ref, kv_ref, hot_ref, bias_ref, dq_ref, keep_ref, give_ref,
                acc, dpbuf, pbuf, qt, dot_t, qs, dos, stat_m, stat_l, stat_d, dqt):
    r = pl.program_id(0)

    @pl.when(r == 0)
    def _():
        acc[...] = jnp.zeros_like(acc)

    for h in range(GROUP):
        q = qd_ref[:, h * HEAD:(h + 1) * HEAD]
        g = qd_ref[:, (GROUP + h) * HEAD:(GROUP + h + 1) * HEAD]
        qt[h, :HEAD, :] = q.T
        qt[h, HEAD:, :] = bias_ref[0]
        dot_t[h] = g.T
    dqt[...] = jnp.zeros_like(dqt)
    steps = (counts[r] + WIDE - 1) // WIDE

    def blocks(i):
        ids = [lists[r * NB + i * WIDE + j] for j in range(WIDE)]
        real = [jnp.minimum(b, NB - 1) for b in ids]
        return ids, [(b % T, b // T) for b in real]

    def masked_keys(ids, where):
        return jnp.concatenate(
            [jnp.concatenate([kv_ref[t, zq, :, :HEAD], hot_ref[b]], axis=1) for b, (t, zq) in zip(ids, where)],
            axis=0)

    def forward(i, carry):
        ids, where = blocks(i)
        lhs = masked_keys(ids, where)
        v = jnp.concatenate([kv_ref[t, zq, :, HEAD:] for t, zq in where], axis=0)
        for h in range(GROUP):
            cols = slice(h * QT, (h + 1) * QT)
            p = jnp.exp2(dot(lhs, qt[h]) * (SCALE * LOG2E))
            dp = dot(v, dot_t[h])
            stat_l[h] += fold(p, jnp.sum)
            stat_d[h] += fold(p * dp, jnp.sum)
            pbuf[i, :, cols] = p.astype(BF16)
            dpbuf[i, :, cols] = dp
        return carry

    def forward_all():
        stat_l[...] = jnp.zeros_like(stat_l)
        stat_d[...] = jnp.zeros_like(stat_d)
        lax.fori_loop(0, steps, forward, 0)
        return [jnp.sum(stat_l[h], axis=0, keepdims=True) for h in range(GROUP)]

    sums = forward_all()
    least = jnp.min(functools.reduce(jnp.minimum, sums))
    most = jnp.max(functools.reduce(jnp.maximum, sums))

    @pl.when(jnp.logical_not((least > LEAST) & (most < MOST)))
    def _():
        stat_m[...] = jnp.full_like(stat_m, NEG)

        def tops(i, carry):
            lhs = masked_keys(*blocks(i))
            for h in range(GROUP):
                stat_m[h] = jnp.maximum(stat_m[h], fold(dot(lhs, qt[h]), jnp.max))
            return carry

        lax.fori_loop(0, steps, tops, 0)
        for h in range(GROUP):
            top = jnp.max(stat_m[h], axis=0, keepdims=True)
            qt[h, HEAD:, :] = (bias_ref[0].astype(F32) - top).astype(BF16)
        forward_all()

    invs = []
    for h in range(GROUP):
        inv = 1.0 / jnp.sum(stat_l[h], axis=0, keepdims=True)
        delta = jnp.sum(stat_d[h], axis=0, keepdims=True) * inv
        stat_d[h] = jnp.broadcast_to(delta, (8, QT))
        col = jnp.broadcast_to(inv, (HEAD, QT)).T
        q = qd_ref[:, h * HEAD:(h + 1) * HEAD].astype(F32)
        g = qd_ref[:, (GROUP + h) * HEAD:(GROUP + h + 1) * HEAD].astype(F32)
        qs[h * QT:(h + 1) * QT] = (q * (col * SCALE)).astype(BF16)
        dos[h * QT:(h + 1) * QT] = (g * col).astype(BF16)
        invs.append(inv)

    def backward(i, carry):
        _, where = blocks(i)
        k = jnp.concatenate([kv_ref[t, zq, :, :HEAD] for t, zq in where], axis=0)
        dv = dot(pbuf[i], dos[...])
        dss = []
        for h in range(GROUP):
            cols = slice(h * QT, (h + 1) * QT)
            dss.append((pbuf[i, :, cols].astype(F32) * (dpbuf[i, :, cols] - stat_d[h, :1])).astype(BF16))
        ds = jnp.concatenate(dss, axis=1)
        dqt[...] += dot_tn(k, ds)
        dk = dot(ds, qs[...])
        for j, (t, zq) in enumerate(where):
            acc[t, zq, :, :HEAD] += dk[j * BLK:(j + 1) * BLK]
            acc[t, zq, :, HEAD:] += dv[j * BLK:(j + 1) * BLK]
        return carry

    lax.fori_loop(0, steps, backward, 0)
    for h in range(GROUP):
        cols = slice(h * QT, (h + 1) * QT)
        dq_ref[:, h * HEAD:(h + 1) * HEAD] = (dqt[:, cols] * (invs[h] * SCALE)).T.astype(BF16)

    @pl.when(r == NQ - 1)
    def _():
        for i in range(Y):
            keep_ref[i] = acc[i * C + spot[0]].astype(BF16)
            give_ref[i] = acc[i * C + 1 - spot[0]].astype(BF16)


def attention(lists, counts, spot, qd, kv, hot, bias):
    def whole(*shape):
        return pl.BlockSpec(shape, lambda r, *_: (0,) * len(shape))

    return pl.pallas_call(
        attn_kernel,
        grid_spec=pltpu.PrefetchScalarGridSpec(
            num_scalar_prefetch=3,
            grid=(NQ,),
            in_specs=[
                pl.BlockSpec((QT, 2 * GROUP * HEAD), lambda r, *_: (r, 0)),
                whole(T, Z, BLK, 2 * HEAD),
                whole(NB + 1, BLK, HEAD),
                pl.BlockSpec((1, HEAD, QT), lambda r, *_: (r, 0, 0)),
            ],
            out_specs=[
                pl.BlockSpec((QT, GROUP * HEAD), lambda r, *_: (r, 0)),
                whole(Y, Z, BLK, 2 * HEAD),
                whole(Y, Z, BLK, 2 * HEAD),
            ],
            scratch_shapes=[
                pltpu.VMEM((T, Z, BLK, 2 * HEAD), F32),
                pltpu.VMEM((NI, KT, GROUP * QT), F32),
                pltpu.VMEM((NI, KT, GROUP * QT), BF16),
                pltpu.VMEM((GROUP, 2 * HEAD, QT), BF16),
                pltpu.VMEM((GROUP, HEAD, QT), BF16),
                pltpu.VMEM((GROUP * QT, HEAD), BF16),
                pltpu.VMEM((GROUP * QT, HEAD), BF16),
                pltpu.VMEM((GROUP, 8, QT), F32),
                pltpu.VMEM((GROUP, 8, QT), F32),
                pltpu.VMEM((GROUP, 8, QT), F32),
                pltpu.VMEM((HEAD, GROUP * QT), F32),
            ],
        ),
        out_shape=[
            jax.ShapeDtypeStruct((Z * BLK, GROUP * HEAD), BF16),
            jax.ShapeDtypeStruct((Y, Z, BLK, 2 * HEAD), BF16),
            jax.ShapeDtypeStruct((Y, Z, BLK, 2 * HEAD), BF16),
        ],
        compiler_params=pltpu.CompilerParams(
            dimension_semantics=("arbitrary",), vmem_limit_bytes=62 * 1024 * 1024
        ),
    )(lists, counts, spot, qd, kv, hot, bias)


def masks(token_span, visible, t_index):
    spans = token_span.reshape(Z, T, BLK)
    n_spans = visible.shape[0]
    lanes = jnp.arange(HEAD, dtype=jnp.int32)
    empty = jnp.full((1, BLK), n_spans, jnp.int32)
    padded = jnp.concatenate([token_span.reshape(NB, BLK), empty], axis=0)
    hot = (padded[..., None] == lanes).astype(BF16)
    mine = lax.dynamic_index_in_dim(spans, t_index, 1, keepdims=False).reshape(NQ, QT)
    span_ids = jnp.arange(n_spans, dtype=jnp.int32)
    mine_hot = (mine[..., None] == span_ids).astype(F32)
    seen = jnp.einsum("rqs,sk->rkq", mine_hot, visible.astype(F32)) > 0
    bias = jnp.where(seen, 0.0, NEG).astype(BF16)
    bias = jnp.pad(bias, ((0, 0), (0, HEAD - n_spans), (0, 0)), constant_values=NEG)
    key_has = jnp.any(token_span.reshape(NB, BLK)[..., None] == span_ids, axis=1)
    seen_any = jnp.any(seen, axis=2)
    used = jnp.any(key_has[None] & seen_any[:, None], axis=2)
    counts = jnp.sum(used.astype(jnp.int32), axis=1)
    ids = jnp.arange(NB, dtype=jnp.int32)
    rank = jnp.sum((used[:, None, :] & (ids[None, :] <= ids[:, None])).astype(jnp.int32), axis=2) - 1
    here = used[:, None, :] & (rank[:, None, :] == ids[:, None])
    lists = jnp.sum(jnp.where(here, ids, 0), axis=2) + jnp.where(ids >= counts[:, None], NB, 0)
    return hot, bias, lists.reshape(-1).astype(jnp.int32), counts


def per_device(query_rows, key_rows, value_rows, out_grad, token_span, visible):
    core = lax.axis_index("core")
    hot, bias, lists, counts = masks(token_span, visible, lax.axis_index("y") * C + core)

    def by_head(x, y):
        m, n = x.shape[1] // Z, y.shape[1] // Z
        return jnp.stack([jnp.concatenate([x[:, c * m:(c + 1) * m], y[:, c * n:(c + 1) * n]], axis=1) for c in range(Z)])

    def swap(x, axis="z"):
        return lax.all_to_all(x, axis, 0, 0, tiled=True)

    def turn(x):
        me = lax.axis_index("z")
        parts = [lax.dynamic_index_in_dim(x, me, 0, keepdims=False)]
        for k in range(1, Z):
            part = lax.dynamic_index_in_dim(x, (me + k) % Z, 0, keepdims=False)
            parts.append(lax.ppermute(part, "z", [(i, (i + k) % Z) for i in range(Z)]))
        return parts

    def in_order(parts):
        me = lax.axis_index("z")
        parts = jnp.stack(parts)
        return [lax.dynamic_index_in_dim(parts, (me - c) % Z, 0, keepdims=False) for c in range(Z)]

    kv = lax.all_gather(swap(by_head(key_rows, value_rows)), ("y", "core"), axis=0)
    qd = swap(by_head(query_rows, out_grad)).reshape(Z * BLK, -1)
    dq, keep, give = attention(lists, counts, core.reshape(1), qd, kv, hot, bias)
    dq = turn(dq.reshape(Z, BLK, GROUP * HEAD))
    other = lax.ppermute(give, "core", [(0, 1), (1, 0)])
    dkv = swap((keep.astype(F32) + other.astype(F32)).astype(BF16), "y")
    dkv, dq = lax.optimization_barrier((dkv, dq))
    dkv = swap(jnp.sum(dkv.astype(F32), axis=0).astype(BF16))
    dq = jnp.concatenate(in_order(dq), axis=1)
    dk = jnp.concatenate([dkv[c, :, :HEAD] for c in range(Z)], axis=1)
    dv = jnp.concatenate([dkv[c, :, HEAD:] for c in range(Z)], axis=1)
    return dq, dk, dv


def solution(mesh):
    dp = mesh.shape["dp"]
    split = Mesh(mesh.devices.reshape(Z, Y, C, dp), ("z", "y", "core", "dp"))
    rows = P(("dp", "z", "y", "core"), None)
    return jax.shard_map(
        per_device,
        mesh=split,
        in_specs=(rows, rows, rows, rows, P("dp"), P("dp", None)),
        out_specs=(rows, rows, rows),
        check_vma=False,
    )
```

time: 187 us -> 190 us (1.016)
  the two profiles are of different devices: /device:TPU:2 before, /device:TPU:4 now
where the time goes in v2:
time: 190 us
  Pallas kernels  52.8 us (28%)
  starting transfers between devices  43.1 us (23%)
  waiting for transfers between devices  41.1 us (22%)
  blocking collectives  22.3 us (12%)
  between operations  14.2 us (7%)
  other arithmetic  11.6 us (6%)
  local copies, waits for them, and re-layouts  4.68 us (2%)
    pallas_call x1, Pallas kernels, attention(): pl.pallas_call(attn_kernel, grid_spec=pltpu.PrefetchScalarGridSpec(num_sc...  52.8 us
    all_to_all x3, starting transfers between devices, swap(): return lax.all_to_all(x, axis, 0, 0, tiled=True)  30.2 us
    all_to_all x3, waiting for transfers between devices, swap(): return lax.all_to_all(x, axis, 0, 0, tiled=True)  27.2 us
    all_to_all x1, blocking collectives, swap(): return lax.all_to_all(x, axis, 0, 0, tiled=True)  22.3 us
    ppermute x3, waiting for transfers between devices, turn(): parts.append(lax.ppermute(part, 'z', [(i, (i + k) % Z) for i in range(Z)]))  10.4 us
    ppermute x3, starting transfers between devices, turn(): parts.append(lax.ppermute(part, 'z', [(i, (i + k) % Z) for i in range(Z)]))  10.4 us
  transfers between devices with their start and end apart: 8, of which 8 were waited for; matrix products, arithmetic and copies ran while one was open for 4% of the time, Pallas kernels for 0%

profile of v2, /device:TPU:4, one launch (start us, length us, event | category | flops | bytes accessed | tf_op | source)
XLA Modules:
  0.0 190.2 jit_solution(15140044419038823265)
XLA Ops:
  7.2 0.9 fusion.9
  8.1 1.0 fusion.10
  9.2 22.3 %all_to_all.20 = bf16[4,192,256]{2,1,0:T(8,128)(2,1)} all-to-all(bf16[4,192,256]{2,1,0:T(8,128)(2,1)S(1)} %pad_maximum_fusion.3), channel_id=1, replica_groups=mesh['z'=4,'y'=4,'core'=2,'dp'=8] {'z'}, dimensions={0} | all-to-all | bytes 786432 | tf_op jit(solution)/shard_map/all_to_all | solution.py:230
  31.9 1.2 pad_maximum_fusion
  33.1 3.7 %all-to-all-start = ((bf16[4,192,768]{2,1,0:T(8,128)(2,1)}), bf16[4,192,768]{2,1,0:T(8,128)(2,1)S(1)}, u32[]{:S(2)}, u32[]{:S(2)}) async-start(bf16[4,192,768]{2,1,0:T(8,128)(2,1)} %pad_maximum_fusion), calls=%async_computation | async-start | bytes 2359296 | tf_op jit(solution)/shard_map/all_to_all | solution.py:230
  36.8 0.6 fusion.2
  37.7 0.3 fusion.11
  38.3 0.1 convert_reduce_fusion
  38.5 0.2 select_reduce_fusion
  38.7 0.6 add.88.lists
  39.3 0.7 pad.5.bias_ref
  40.0 2.5 %fusion.hot_ref = bf16[33,192,128]{2,1,0:T(8,128)(2,1)} fusion(s32[33,192]{1,0:T(8,128)S(1)} %concatenate.44), kind=kLoop, calls=%fused_computation.1 | loop fusion | flops 1622016 | bytes 1647360 | tf_op jit(solution)/shard_map/convert_element_type | solution.py:203
  42.5 16.5 %all-to-all-done = bf16[4,192,768]{2,1,0:T(8,128)(2,1)S(1)} async-done(((bf16[4,192,768]{2,1,0:T(8,128)(2,1)}), bf16[4,192,768]{2,1,0:T(8,128)(2,1)S(1)}, u32[]{:S(2)}, u32[]{:S(2)}) %all-to-all-start) | async-done | bytes 1179680 | tf_op jit(solution)/shard_map/all_to_all | solution.py:230
  59.0 0.3 all-gather.3.cloned.1.call-done
  59.2 0.8 copy-done
  60.1 52.8 %shard_map.85 = (bf16[768,384]{1,0:T(8,128)(2,1)}, bf16[4,4,192,256]{3,2,1,0:T(8,128)(2,1)}, bf16[4,4,192,256]{3,2,1,0:T(8,128)(2,1)}) custom-call(s32[96]{0:T(128)} %add.88.lists, s32[3]{0:T(128)} %copy-done.5, s32[1]{0:T(128)} %bitcast.2.spot, bf16[768,768]{1,0:T(8,128)(2,1)} %bitcast.63, bf16[8,4,192,256]{3,2,1,0:T(8,128)(2,1)} %bitcast.64, ...), custom_call_target="tpu_custom_call" | custom-call | tf_op jit(solution)/shard_map/pallas_call | solution.py:156
  112.8 2.4 %collective-permute-start = (bf16[4,4,192,256]{3,2,1,0:T(8,128)(2,1)}, bf16[4,4,192,256]{3,2,1,0:T(8,128)(2,1)S(1)}, u32[]{:S(2)}, u32[]{:S(2)}) collective-permute-start(bf16[4,4,192,256]{3,2,1,0:T(8,128)(2,1)} %get-tuple-element.12), channel_id=1, source_target_pairs={{0,8},{8,0},{1,9},{9,1},{2,10},{10,2},{3,11},{11,3},{4,12},{12,4},... | collective-permute-start | bytes 4718600 | tf_op jit(solution)/shard_map/ppermute | solution.py:249
  115.3 3.2 %collective-permute-done = bf16[4,4,192,256]{3,2,1,0:T(8,128)(2,1)S(1)} collective-permute-done((bf16[4,4,192,256]{3,2,1,0:T(8,128)(2,1)}, bf16[4,4,192,256]{3,2,1,0:T(8,128)(2,1)S(1)}, u32[]{:S(2)}, u32[]{:S(2)}) %collective-permute-start) | collective-permute-done | bytes 1572896 | tf_op jit(solution)/shard_map/ppermute | solution.py:249
  118.5 3.1 %add_convert_fusion = bf16[4,4,192,256]{3,2,1,0:T(8,128)(2,1)} fusion(bf16[4,4,192,256]{3,2,1,0:T(8,128)(2,1)S(1)} %collective-permute-done, bf16[4,4,192,256]{3,2,1,0:T(8,128)(2,1)} %get-tuple-element.11), kind=kLoop, calls=%fused_computation.2 | loop fusion | flops 3145728 | bytes 4718592 | tf_op jit(solution)/shard_map/convert_element_type | solution.py:250
  121.6 17.4 %all-to-all-start.2 = ((bf16[4,4,192,256]{3,2,1,0:T(8,128)(2,1)}), bf16[4,4,192,256]{3,2,1,0:T(8,128)(2,1)S(1)}, u32[]{:S(2)}, u32[]{:S(2)}) async-start(bf16[4,4,192,256]{3,2,1,0:T(8,128)(2,1)} %add_convert_fusion), calls=%async_computation.2 | async-start | bytes 3145728 | tf_op jit(solution)/shard_map/all_to_all | solution.py:230
  139.1 6.1 %collective-permute-start.1 = (bf16[192,384]{1,0:T(8,128)(2,1)S(1)}, bf16[192,384]{1,0:T(8,128)(2,1)S(1)}, u32[]{:S(2)}, u32[]{:S(2)}) collective-permute-start(bf16[192,384]{1,0:T(8,128)(2,1)S(1)} %get-tuple-element.25), channel_id=1, source_target_pairs={{0,64},{64,128},{128,192},{192,0},{1,65},{65,129},{129,193},{193,1... | collective-permute-start | bytes 442376 | tf_op jit(solution)/shard_map/ppermute | solution.py:237
  145.2 4.2 %collective-permute-start.2 = (bf16[192,384]{1,0:T(8,128)(2,1)S(1)}, bf16[192,384]{1,0:T(8,128)(2,1)S(1)}, u32[]{:S(2)}, u32[]{:S(2)}) collective-permute-start(bf16[192,384]{1,0:T(8,128)(2,1)S(1)} %get-tuple-element.24), channel_id=1, source_target_pairs={{0,128},{64,192},{128,0},{192,64},{1,129},{65,193},{129,1},{193,65... | collective-permute-start | bytes 442376 | tf_op jit(solution)/shard_map/ppermute | solution.py:237
  149.4 2.3 %collective-permute-done.1 = bf16[192,384]{1,0:T(8,128)(2,1)S(1)} collective-permute-done((bf16[192,384]{1,0:T(8,128)(2,1)S(1)}, bf16[192,384]{1,0:T(8,128)(2,1)S(1)}, u32[]{:S(2)}, u32[]{:S(2)}) %collective-permute-start.1) | collective-permute-done | bytes 147488 | tf_op jit(solution)/shard_map/ppermute | solution.py:237
  151.7 7.6 %collective-permute-done.2 = bf16[192,384]{1,0:T(8,128)(2,1)S(1)} collective-permute-done((bf16[192,384]{1,0:T(8,128)(2,1)S(1)}, bf16[192,384]{1,0:T(8,128)(2,1)S(1)}, u32[]{:S(2)}, u32[]{:S(2)}) %collective-permute-start.2) | collective-permute-done | bytes 147488 | tf_op jit(solution)/shard_map/ppermute | solution.py:237
  159.3 0.5 collective-permute-done.3
  159.8 0.2 all-to-all-done.2
  160.0 1.1 reduce_sum.42
  161.1 9.2 %all-to-all-start.3 = ((bf16[4,192,256]{2,1,0:T(8,128)(2,1)}), bf16[4,192,256]{2,1,0:T(8,128)(2,1)S(1)}, u32[]{:S(2)}, u32[]{:S(2)}) async-start(bf16[4,192,256]{2,1,0:T(8,128)(2,1)} %reduce_sum.42), calls=%async_computation.3 | async-start | bytes 786432 | tf_op jit(solution)/shard_map/all_to_all | solution.py:230
  170.5 0.9 pad_maximum_fusion.2
  171.3 10.5 %all-to-all-done.3 = bf16[4,192,256]{2,1,0:T(8,128)(2,1)S(1)} async-done(((bf16[4,192,256]{2,1,0:T(8,128)(2,1)}), bf16[4,192,256]{2,1,0:T(8,128)(2,1)S(1)}, u32[]{:S(2)}, u32[]{:S(2)}) %all-to-all-start.3) | async-done | bytes 393248 | tf_op jit(solution)/shard_map/all_to_all | solution.py:230
  181.9 0.7 pad_maximum_fusion.5
  182.6 0.7 pad_maximum_fusion.4
  (39 shorter events, 1.4 us)
Async XLA Ops:
  7.2 52.1 %all-gather.3.cloned.1.call-start = ((), (), s32[]{:S(2)}) async-start(), calls=%async_computation.4 | async-start | bytes 3538944 | tf_op jit(solution)/shard_map/all_gather | solution.py:245
  8.1 23.5 %copy-start.1 = (bf16[192,1536]{1,0:T(8,128)(2,1)S(1)}, bf16[192,1536]{1,0:T(8,128)(2,1)}, u32[]{:S(2)}) copy-start(bf16[192,1536]{1,0:T(8,128)(2,1)} %param.6) | copy-start | bytes 1769476
  9.1 22.5 %copy-start.2 = (bf16[192,1536]{1,0:T(8,128)(2,1)S(1)}, bf16[192,1536]{1,0:T(8,128)(2,1)}, u32[]{:S(2)}) copy-start(bf16[192,1536]{1,0:T(8,128)(2,1)} %param.9) | copy-start | bytes 1769476
  33.1 3.7 %copy-start.4 = (s32[6144]{0:T(1024)S(1)}, s32[6144]{0:T(1024)}, u32[]{:S(2)}) copy-start(s32[6144]{0:T(1024)} %param.10) | copy-start | bytes 73732
  33.1 4.7 %copy-start.6 = (s32[16,16]{1,0:T(8,128)S(1)}, s32[16,16]{1,0:T(8,128)}, u32[]{:S(2)}) copy-start(s32[16,16]{1,0:T(8,128)} %param.11) | copy-start | bytes 3076
  33.1 25.9 %all-to-all-start = ((bf16[4,192,768]{2,1,0:T(8,128)(2,1)}), bf16[4,192,768]{2,1,0:T(8,128)(2,1)S(1)}, u32[]{:S(2)}, u32[]{:S(2)}) async-start(bf16[4,192,768]{2,1,0:T(8,128)(2,1)} %pad_maximum_fusion), calls=%async_computation | async-start | bytes 2359296 | tf_op jit(solution)/shard_map/all_to_all | solution.py:230
  38.3 20.9 %copy-start.5 = (s32[3]{0:T(128)}, s32[3]{0:T(128)S(1)}, u32[]{:S(2)}) copy-start(s32[3]{0:T(128)S(1)} %convert_reduce_fusion.1.counts) | copy-start | bytes 40
  59.0 1.1 copy-start
  112.8 5.7 %collective-permute-start = (bf16[4,4,192,256]{3,2,1,0:T(8,128)(2,1)}, bf16[4,4,192,256]{3,2,1,0:T(8,128)(2,1)S(1)}, u32[]{:S(2)}, u32[]{:S(2)}) collective-permute-start(bf16[4,4,192,256]{3,2,1,0:T(8,128)(2,1)} %get-tuple-element.12), channel_id=1, source_target_pairs={{0,8},{8,0},{1,9},{9,1},{2,10},{10,2},{3,11},{11,3},{4,12},{12,4},... | collective-permute-start | bytes 4718600 | tf_op jit(solution)/shard_map/ppermute | solution.py:249
  121.6 17.4 %copy-start.3 = (bf16[768,384]{1,0:T(8,128)(2,1)S(1)}, bf16[768,384]{1,0:T(8,128)(2,1)}, u32[]{:S(2)}) copy-start(bf16[768,384]{1,0:T(8,128)(2,1)} %get-tuple-element.13) | copy-start | bytes 1769476
  121.6 38.4 %all-to-all-start.2 = ((bf16[4,4,192,256]{3,2,1,0:T(8,128)(2,1)}), bf16[4,4,192,256]{3,2,1,0:T(8,128)(2,1)S(1)}, u32[]{:S(2)}, u32[]{:S(2)}) async-start(bf16[4,4,192,256]{3,2,1,0:T(8,128)(2,1)} %add_convert_fusion), calls=%async_computation.2 | async-start | bytes 3145728 | tf_op jit(solution)/shard_map/all_to_all | solution.py:230
  139.1 12.7 %collective-permute-start.1 = (bf16[192,384]{1,0:T(8,128)(2,1)S(1)}, bf16[192,384]{1,0:T(8,128)(2,1)S(1)}, u32[]{:S(2)}, u32[]{:S(2)}) collective-permute-start(bf16[192,384]{1,0:T(8,128)(2,1)S(1)} %get-tuple-element.25), channel_id=1, source_target_pairs={{0,64},{64,128},{128,192},{192,0},{1,65},{65,129},{129,193},{193,1... | collective-permute-start | bytes 442376 | tf_op jit(solution)/shard_map/ppermute | solution.py:237
  145.2 14.1 %collective-permute-start.2 = (bf16[192,384]{1,0:T(8,128)(2,1)S(1)}, bf16[192,384]{1,0:T(8,128)(2,1)S(1)}, u32[]{:S(2)}, u32[]{:S(2)}) collective-permute-start(bf16[192,384]{1,0:T(8,128)(2,1)S(1)} %get-tuple-element.24), channel_id=1, source_target_pairs={{0,128},{64,192},{128,0},{192,64},{1,129},{65,193},{129,1},{193,65... | collective-permute-start | bytes 442376 | tf_op jit(solution)/shard_map/ppermute | solution.py:237
  149.4 10.4 %collective-permute-start.3 = (bf16[192,384]{1,0:T(8,128)(2,1)S(1)}, bf16[192,384]{1,0:T(8,128)(2,1)S(1)}, u32[]{:S(2)}, u32[]{:S(2)}) collective-permute-start(bf16[192,384]{1,0:T(8,128)(2,1)S(1)} %get-tuple-element.23), channel_id=1, source_target_pairs={{0,192},{64,0},{128,64},{192,128},{1,193},{65,1},{129,65},{193,129... | collective-permute-start | bytes 442376 | tf_op jit(solution)/shard_map/ppermute | solution.py:237
  161.1 20.7 %all-to-all-start.3 = ((bf16[4,192,256]{2,1,0:T(8,128)(2,1)}), bf16[4,192,256]{2,1,0:T(8,128)(2,1)S(1)}, u32[]{:S(2)}, u32[]{:S(2)}) async-start(bf16[4,192,256]{2,1,0:T(8,128)(2,1)} %reduce_sum.42), calls=%async_computation.3 | async-start | bytes 786432 | tf_op jit(solution)/shard_map/all_to_all | solution.py:230
Sparse Core Ops, SparseCore 0:
  31.7 27.4 all-gather.2

commit v3 on v2

--- a/solution.py
+++ b/solution.py
@@ -15,6 +15,7 @@
 SCALE = HEAD ** -0.5
 LOG2E = 1.4426950408889634
 NEG = -1e30
+LIMIT = 48
 LEAST = 2.0 ** -60
 MOST = 2.0 ** 60
 Z, Y, C = 4, 4, 2
@@ -42,9 +43,10 @@
     return op(x.reshape(x.shape[0] // 8, 8, x.shape[1]), axis=0)
 
 
-def attn_kernel(lists, counts, spot, qd_ref, kv_ref, hot_ref, bias_ref, dq_ref, keep_ref, give_ref,
+def attn_kernel(lists, counts, spot, qd_all, kv_ref, hot_ref, bias_ref, dq_ref, keep_ref, give_ref,
                 acc, dpbuf, pbuf, qt, dot_t, qs, dos, stat_m, stat_l, stat_d, dqt):
     r = pl.program_id(0)
+    qd_ref = qd_all.at[pl.ds(pl.multiple_of(r * QT, QT), QT)]
 
     @pl.when(r == 0)
     def _():
@@ -54,7 +56,7 @@
         q = qd_ref[:, h * HEAD:(h + 1) * HEAD]
         g = qd_ref[:, (GROUP + h) * HEAD:(GROUP + h + 1) * HEAD]
         qt[h, :HEAD, :] = q.T
-        qt[h, HEAD:, :] = bias_ref[0]
+        qt[h, HEAD:, :] = bias_ref[r]
         dot_t[h] = g.T
     dqt[...] = jnp.zeros_like(dqt)
     steps = (counts[r] + WIDE - 1) // WIDE
@@ -106,7 +108,7 @@
         lax.fori_loop(0, steps, tops, 0)
         for h in range(GROUP):
             top = jnp.max(stat_m[h], axis=0, keepdims=True)
-            qt[h, HEAD:, :] = (bias_ref[0].astype(F32) - top).astype(BF16)
+            qt[h, HEAD:, :] = (bias_ref[r].astype(F32) - top).astype(BF16)
         forward_all()
 
     invs = []
@@ -138,9 +140,18 @@
         return carry
 
     lax.fori_loop(0, steps, backward, 0)
-    for h in range(GROUP):
-        cols = slice(h * QT, (h + 1) * QT)
-        dq_ref[:, h * HEAD:(h + 1) * HEAD] = (dqt[:, cols] * (invs[h] * SCALE)).T.astype(BF16)
+    for tile in range(NQ):
+        @pl.when(r == tile)
+        def _():
+            for h in range(GROUP):
+                cols = slice(h * QT, (h + 1) * QT)
+                dq = (dqt[:, cols] * (invs[h] * SCALE)).T.astype(BF16)
+                row = 0
+                while row < QT:
+                    q, start = divmod(tile * QT + row, BLK)
+                    take = min(BLK - start, QT - row)
+                    dq_ref[(q + Z - spot[1]) % Z, start:start + take, h * HEAD:(h + 1) * HEAD] = dq[row:row + take]
+                    row += take
 
     @pl.when(r == NQ - 1)
     def _():
@@ -150,25 +161,14 @@
 
 
 def attention(lists, counts, spot, qd, kv, hot, bias):
-    def whole(*shape):
-        return pl.BlockSpec(shape, lambda r, *_: (0,) * len(shape))
-
+    vmem = pl.BlockSpec(memory_space=pltpu.VMEM)
     return pl.pallas_call(
         attn_kernel,
         grid_spec=pltpu.PrefetchScalarGridSpec(
             num_scalar_prefetch=3,
             grid=(NQ,),
-            in_specs=[
-                pl.BlockSpec((QT, 2 * GROUP * HEAD), lambda r, *_: (r, 0)),
-                whole(T, Z, BLK, 2 * HEAD),
-                whole(NB + 1, BLK, HEAD),
-                pl.BlockSpec((1, HEAD, QT), lambda r, *_: (r, 0, 0)),
-            ],
-            out_specs=[
-                pl.BlockSpec((QT, GROUP * HEAD), lambda r, *_: (r, 0)),
-                whole(Y, Z, BLK, 2 * HEAD),
-                whole(Y, Z, BLK, 2 * HEAD),
-            ],
+            in_specs=[vmem] * 4,
+            out_specs=[vmem] * 3,
             scratch_shapes=[
                 pltpu.VMEM((T, Z, BLK, 2 * HEAD), F32),
                 pltpu.VMEM((NI, KT, GROUP * QT), F32),
@@ -184,12 +184,12 @@
             ],
         ),
         out_shape=[
-            jax.ShapeDtypeStruct((Z * BLK, GROUP * HEAD), BF16),
+            jax.ShapeDtypeStruct((Z, BLK, GROUP * HEAD), BF16),
             jax.ShapeDtypeStruct((Y, Z, BLK, 2 * HEAD), BF16),
             jax.ShapeDtypeStruct((Y, Z, BLK, 2 * HEAD), BF16),
         ],
         compiler_params=pltpu.CompilerParams(
-            dimension_semantics=("arbitrary",), vmem_limit_bytes=62 * 1024 * 1024
+            dimension_semantics=("arbitrary",), vmem_limit_bytes=LIMIT * 1024 * 1024
         ),
     )(lists, counts, spot, qd, kv, hot, bias)
 
@@ -230,12 +230,7 @@
         return lax.all_to_all(x, axis, 0, 0, tiled=True)
 
     def turn(x):
-        me = lax.axis_index("z")
-        parts = [lax.dynamic_index_in_dim(x, me, 0, keepdims=False)]
-        for k in range(1, Z):
-            part = lax.dynamic_index_in_dim(x, (me + k) % Z, 0, keepdims=False)
-            parts.append(lax.ppermute(part, "z", [(i, (i + k) % Z) for i in range(Z)]))
-        return parts
+        return [x[0]] + [lax.ppermute(x[k], "z", [(i, (i + k) % Z) for i in range(Z)]) for k in range(1, Z)]
 
     def in_order(parts):
         me = lax.axis_index("z")
@@ -244,8 +239,8 @@
 
     kv = lax.all_gather(swap(by_head(key_rows, value_rows)), ("y", "core"), axis=0)
     qd = swap(by_head(query_rows, out_grad)).reshape(Z * BLK, -1)
-    dq, keep, give = attention(lists, counts, core.reshape(1), qd, kv, hot, bias)
-    dq = turn(dq.reshape(Z, BLK, GROUP * HEAD))
+    dq, keep, give = attention(lists, counts, jnp.stack([core, lax.axis_index("z")]), qd, kv, hot, bias)
+    dq = turn(dq)
     other = lax.ppermute(give, "core", [(0, 1), (1, 0)])
     dkv = swap((keep.astype(F32) + other.astype(F32)).astype(BF16), "y")
     dkv, dq = lax.optimization_barrier((dkv, dq))

time: 190 us -> 185 us (0.974)
  the two profiles are of different devices: /device:TPU:4 before, /device:TPU:2 now
where the time goes in v3:
time: 185 us; the launch traced here: 184 us
  Pallas kernels  50.7 us (27%)
  waiting for transfers between devices  44.1 us (24%)
  starting transfers between devices  38.9 us (21%)
  blocking collectives  22.3 us (12%)
  between operations  14.2 us (8%)
  other arithmetic  10.3 us (6%)
  local copies, waits for them, and re-layouts  2.64 us (1%)
    pallas_call x1, Pallas kernels, attention(): pl.pallas_call(attn_kernel, grid_spec=pltpu.PrefetchScalarGridSpec(num_sc...  50.7 us
    all_to_all x3, waiting for transfers between devices, swap(): return lax.all_to_all(x, axis, 0, 0, tiled=True)  31.3 us
    all_to_all x3, starting transfers between devices, swap(): return lax.all_to_all(x, axis, 0, 0, tiled=True)  28.6 us
    all_to_all x1, blocking collectives, swap(): return lax.all_to_all(x, axis, 0, 0, tiled=True)  22.3 us
    ppermute x3, starting transfers between devices, turn(): lax.ppermute(x[k], 'z', [(i, (i + k) % Z) for i in range(Z)])  9.9 us
    ppermute x3, waiting for transfers between devices, turn(): lax.ppermute(x[k], 'z', [(i, (i + k) % Z) for i in range(Z)])  9.39 us
  transfers between devices with their start and end apart: 8, of which 7 were waited for; matrix products, arithmetic and copies ran while one was open for 4% of the time, Pallas kernels for 0%

profile of v3, /device:TPU:2, one launch (start us, length us, event | category | flops | bytes accessed | tf_op | source)
XLA Modules:
  0.0 183.6 jit_solution(7532086153385325476)
XLA Ops:
  7.2 0.9 fusion.9
  8.1 1.0 fusion.10
  9.2 22.3 %all_to_all.20 = bf16[4,192,256]{2,1,0:T(8,128)(2,1)} all-to-all(bf16[4,192,256]{2,1,0:T(8,128)(2,1)S(1)} %pad_maximum_fusion.3), channel_id=1, replica_groups=mesh['z'=4,'y'=4,'core'=2,'dp'=8] {'z'}, dimensions={0} | all-to-all | bytes 786432 | tf_op jit(solution)/shard_map/all_to_all | solution.py:230
  31.9 1.2 pad_maximum_fusion
  33.1 3.7 %all-to-all-start = ((bf16[4,192,768]{2,1,0:T(8,128)(2,1)}), bf16[4,192,768]{2,1,0:T(8,128)(2,1)S(1)}, u32[]{:S(2)}, u32[]{:S(2)}) async-start(bf16[4,192,768]{2,1,0:T(8,128)(2,1)} %pad_maximum_fusion), calls=%async_computation | async-start | bytes 2359296 | tf_op jit(solution)/shard_map/all_to_all | solution.py:230
  37.0 0.6 fusion.2
  37.7 0.3 fusion.11
  38.1 0.1 and_reduce_fusion
  38.2 0.1 convert_reduce_fusion.1.counts
  38.3 0.2 convert_reduce_fusion
  38.5 0.2 select_reduce_fusion
  38.9 2.5 %fusion.hot_ref = bf16[33,192,128]{2,1,0:T(8,128)(2,1)} fusion(s32[33,192]{1,0:T(8,128)S(1)} %concatenate.44), kind=kLoop, calls=%fused_computation.1 | loop fusion | flops 1622016 | bytes 1647360 | tf_op jit(solution)/shard_map/convert_element_type | solution.py:203
  41.4 17.6 %all-to-all-done = bf16[4,192,768]{2,1,0:T(8,128)(2,1)S(1)} async-done(((bf16[4,192,768]{2,1,0:T(8,128)(2,1)}), bf16[4,192,768]{2,1,0:T(8,128)(2,1)S(1)}, u32[]{:S(2)}, u32[]{:S(2)}) %all-to-all-start) | async-done | bytes 1179680 | tf_op jit(solution)/shard_map/all_to_all | solution.py:230
  59.0 0.3 all-gather.3.cloned.1.call-done
  59.3 50.7 %shard_map.85 = (bf16[4,192,384]{2,1,0:T(8,128)(2,1)S(1)}, bf16[4,4,192,256]{3,2,1,0:T(8,128)(2,1)S(1)}, bf16[4,4,192,256]{3,2,1,0:T(8,128)(2,1)S(1)}) custom-call(s32[96]{0:T(128)S(1)} %add.58.lists, s32[3]{0:T(128)S(1)} %convert_reduce_fusion.1.counts, s32[2]{0:T(128)S(1)} %pad_add_fusion.spot, bf16[768,768]{1,0:T(8,128)(2,1)S(1)} %bitcast.63, ...), custom_call_target="tpu_custom_call" | custom-call | tf_op jit(solution)/shard_map/pallas_call | solution.py:165
  109.9 0.3 collective-permute-start
  110.3 3.2 %collective-permute-done = bf16[4,4,192,256]{3,2,1,0:T(8,128)(2,1)S(1)} collective-permute-done((bf16[4,4,192,256]{3,2,1,0:T(8,128)(2,1)S(1)}, bf16[4,4,192,256]{3,2,1,0:T(8,128)(2,1)S(1)}, u32[]{:S(2)}, u32[]{:S(2)}) %collective-permute-start) | collective-permute-done | bytes 1572896 | tf_op jit(solution)/shard_map/ppermute | solution.py:244
  113.4 1.6 add_convert_fusion
  115.1 17.8 %all-to-all-start.2 = ((bf16[4,4,192,256]{3,2,1,0:T(8,128)(2,1)}), bf16[4,4,192,256]{3,2,1,0:T(8,128)(2,1)S(1)}, u32[]{:S(2)}, u32[]{:S(2)}) async-start(bf16[4,4,192,256]{3,2,1,0:T(8,128)(2,1)} %add_convert_fusion), calls=%async_computation.2 | async-start | bytes 3145728 | tf_op jit(solution)/shard_map/all_to_all | solution.py:230
  132.9 4.3 %collective-permute-start.1 = (bf16[192,384]{1,0:T(8,128)(2,1)S(1)}, bf16[192,384]{1,0:T(8,128)(2,1)S(1)}, u32[]{:S(2)}, u32[]{:S(2)}) collective-permute-start(bf16[192,384]{1,0:T(8,128)(2,1)S(1)} %get-tuple-element.25), channel_id=1, source_target_pairs={{0,64},{64,128},{128,192},{192,0},{1,65},{65,129},{129,193},{193,1... | collective-permute-start | bytes 442376 | tf_op jit(solution)/shard_map/ppermute | solution.py:233
  137.3 4.2 %collective-permute-start.2 = (bf16[192,384]{1,0:T(8,128)(2,1)S(1)}, bf16[192,384]{1,0:T(8,128)(2,1)S(1)}, u32[]{:S(2)}, u32[]{:S(2)}) collective-permute-start(bf16[192,384]{1,0:T(8,128)(2,1)S(1)} %get-tuple-element.24), channel_id=1, source_target_pairs={{0,128},{64,192},{128,0},{192,64},{1,129},{65,193},{129,1},{193,65... | collective-permute-start | bytes 442376 | tf_op jit(solution)/shard_map/ppermute | solution.py:233
  141.5 1.3 collective-permute-start.3
  142.8 0.2 collective-permute-done.1
  143.0 9.2 %collective-permute-done.2 = bf16[192,384]{1,0:T(8,128)(2,1)S(1)} collective-permute-done((bf16[192,384]{1,0:T(8,128)(2,1)S(1)}, bf16[192,384]{1,0:T(8,128)(2,1)S(1)}, u32[]{:S(2)}, u32[]{:S(2)}) %collective-permute-start.2) | collective-permute-done | bytes 147488 | tf_op jit(solution)/shard_map/ppermute | solution.py:233
  152.2 1.9 %all-to-all-done.2 = bf16[4,4,192,256]{3,2,1,0:T(8,128)(2,1)S(1)} async-done(((bf16[4,4,192,256]{3,2,1,0:T(8,128)(2,1)}), bf16[4,4,192,256]{3,2,1,0:T(8,128)(2,1)S(1)}, u32[]{:S(2)}, u32[]{:S(2)}) %all-to-all-start.2) | async-done | bytes 1572896 | tf_op jit(solution)/shard_map/all_to_all | solution.py:230
  154.1 1.1 reduce_sum.42
  155.2 7.2 %all-to-all-start.3 = ((bf16[4,192,256]{2,1,0:T(8,128)(2,1)}), bf16[4,192,256]{2,1,0:T(8,128)(2,1)S(1)}, u32[]{:S(2)}, u32[]{:S(2)}) async-start(bf16[4,192,256]{2,1,0:T(8,128)(2,1)} %reduce_sum.42), calls=%async_computation.3 | async-start | bytes 786432 | tf_op jit(solution)/shard_map/all_to_all | solution.py:230
  162.4 0.1 pad_maximum_fusion.1
  162.6 0.9 pad_maximum_fusion.2
  163.4 11.8 %all-to-all-done.3 = bf16[4,192,256]{2,1,0:T(8,128)(2,1)S(1)} async-done(((bf16[4,192,256]{2,1,0:T(8,128)(2,1)}), bf16[4,192,256]{2,1,0:T(8,128)(2,1)S(1)}, u32[]{:S(2)}, u32[]{:S(2)}) %all-to-all-start.3) | async-done | bytes 393248 | tf_op jit(solution)/shard_map/all_to_all | solution.py:230
  175.3 0.7 pad_maximum_fusion.5
  176.0 0.7 pad_maximum_fusion.4
  (34 shorter events, 1.2 us)
Async XLA Ops:
  7.2 52.1 %all-gather.3.cloned.1.call-start = ((), (), s32[]{:S(2)}) async-start(), calls=%async_computation.4 | async-start | bytes 3538944 | tf_op jit(solution)/shard_map/all_gather | solution.py:240
  8.1 23.5 %copy-start = (bf16[192,1536]{1,0:T(8,128)(2,1)S(1)}, bf16[192,1536]{1,0:T(8,128)(2,1)}, u32[]{:S(2)}) copy-start(bf16[192,1536]{1,0:T(8,128)(2,1)} %param.6) | copy-start | bytes 1769476
  9.1 22.5 %copy-start.1 = (bf16[192,1536]{1,0:T(8,128)(2,1)S(1)}, bf16[192,1536]{1,0:T(8,128)(2,1)}, u32[]{:S(2)}) copy-start(bf16[192,1536]{1,0:T(8,128)(2,1)} %param.9) | copy-start | bytes 1769476
  33.1 3.7 %copy-start.2 = (s32[6144]{0:T(1024)S(1)}, s32[6144]{0:T(1024)}, u32[]{:S(2)}) copy-start(s32[6144]{0:T(1024)} %param.10) | copy-start | bytes 73732
  33.1 4.7 %copy-start.3 = (s32[16,16]{1,0:T(8,128)S(1)}, s32[16,16]{1,0:T(8,128)}, u32[]{:S(2)}) copy-start(s32[16,16]{1,0:T(8,128)} %param.11) | copy-start | bytes 3076
  33.1 25.9 %all-to-all-start = ((bf16[4,192,768]{2,1,0:T(8,128)(2,1)}), bf16[4,192,768]{2,1,0:T(8,128)(2,1)S(1)}, u32[]{:S(2)}, u32[]{:S(2)}) async-start(bf16[4,192,768]{2,1,0:T(8,128)(2,1)} %pad_maximum_fusion), calls=%async_computation | async-start | bytes 2359296 | tf_op jit(solution)/shard_map/all_to_all | solution.py:230
  109.9 3.5 %collective-permute-start = (bf16[4,4,192,256]{3,2,1,0:T(8,128)(2,1)S(1)}, bf16[4,4,192,256]{3,2,1,0:T(8,128)(2,1)S(1)}, u32[]{:S(2)}, u32[]{:S(2)}) collective-permute-start(bf16[4,4,192,256]{3,2,1,0:T(8,128)(2,1)S(1)} %get-tuple-element.12), channel_id=1, source_target_pairs={{0,8},{8,0},{1,9},{9,1},{2,10},{10,2},{3,11},{11,3},{4,12},{12,4},... | collective-permute-start | bytes 4718600 | tf_op jit(solution)/shard_map/ppermute | solution.py:244
  115.1 39.0 %all-to-all-start.2 = ((bf16[4,4,192,256]{3,2,1,0:T(8,128)(2,1)}), bf16[4,4,192,256]{3,2,1,0:T(8,128)(2,1)S(1)}, u32[]{:S(2)}, u32[]{:S(2)}) async-start(bf16[4,4,192,256]{3,2,1,0:T(8,128)(2,1)} %add_convert_fusion), calls=%async_computation.2 | async-start | bytes 3145728 | tf_op jit(solution)/shard_map/all_to_all | solution.py:230
  132.9 10.1 %collective-permute-start.1 = (bf16[192,384]{1,0:T(8,128)(2,1)S(1)}, bf16[192,384]{1,0:T(8,128)(2,1)S(1)}, u32[]{:S(2)}, u32[]{:S(2)}) collective-permute-start(bf16[192,384]{1,0:T(8,128)(2,1)S(1)} %get-tuple-element.25), channel_id=1, source_target_pairs={{0,64},{64,128},{128,192},{192,0},{1,65},{65,129},{129,193},{193,1... | collective-permute-start | bytes 442376 | tf_op jit(solution)/shard_map/ppermute | solution.py:233
  137.3 14.9 %collective-permute-start.2 = (bf16[192,384]{1,0:T(8,128)(2,1)S(1)}, bf16[192,384]{1,0:T(8,128)(2,1)S(1)}, u32[]{:S(2)}, u32[]{:S(2)}) collective-permute-start(bf16[192,384]{1,0:T(8,128)(2,1)S(1)} %get-tuple-element.24), channel_id=1, source_target_pairs={{0,128},{64,192},{128,0},{192,64},{1,129},{65,193},{129,1},{193,65... | collective-permute-start | bytes 442376 | tf_op jit(solution)/shard_map/ppermute | solution.py:233
  141.5 10.7 %collective-permute-start.3 = (bf16[192,384]{1,0:T(8,128)(2,1)S(1)}, bf16[192,384]{1,0:T(8,128)(2,1)S(1)}, u32[]{:S(2)}, u32[]{:S(2)}) collective-permute-start(bf16[192,384]{1,0:T(8,128)(2,1)S(1)} %get-tuple-element.23), channel_id=1, source_target_pairs={{0,192},{64,0},{128,64},{192,128},{1,193},{65,1},{129,65},{193,129... | collective-permute-start | bytes 442376 | tf_op jit(solution)/shard_map/ppermute | solution.py:233
  155.2 20.0 %all-to-all-start.3 = ((bf16[4,192,256]{2,1,0:T(8,128)(2,1)}), bf16[4,192,256]{2,1,0:T(8,128)(2,1)S(1)}, u32[]{:S(2)}, u32[]{:S(2)}) async-start(bf16[4,192,256]{2,1,0:T(8,128)(2,1)} %reduce_sum.42), calls=%async_computation.3 | async-start | bytes 786432 | tf_op jit(solution)/shard_map/all_to_all | solution.py:230
Sparse Core Ops, SparseCore 0:
  31.7 27.5 all-gather.2

commit v4 on v3

--- a/solution.py
+++ b/solution.py
@@ -150,14 +150,15 @@
                 while row < QT:
                     q, start = divmod(tile * QT + row, BLK)
                     take = min(BLK - start, QT - row)
-                    dq_ref[(q + Z - spot[1]) % Z, start:start + take, h * HEAD:(h + 1) * HEAD] = dq[row:row + take]
+                    dq_ref[q, start:start + take, h * HEAD:(h + 1) * HEAD] = dq[row:row + take]
                     row += take
 
     @pl.when(r == NQ - 1)
     def _():
         for i in range(Y):
-            keep_ref[i] = acc[i * C + spot[0]].astype(BF16)
-            give_ref[i] = acc[i * C + 1 - spot[0]].astype(BF16)
+            y = (spot[1] + i) % Y
+            keep_ref[i] = acc[y * C + spot[0]].astype(BF16)
+            give_ref[i] = acc[y * C + 1 - spot[0]].astype(BF16)
 
 
 def attention(lists, counts, spot, qd, kv, hot, bias):
@@ -229,23 +230,20 @@
     def swap(x, axis="z"):
         return lax.all_to_all(x, axis, 0, 0, tiled=True)
 
-    def turn(x):
-        return [x[0]] + [lax.ppermute(x[k], "z", [(i, (i + k) % Z) for i in range(Z)]) for k in range(1, Z)]
-
-    def in_order(parts):
-        me = lax.axis_index("z")
-        parts = jnp.stack(parts)
-        return [lax.dynamic_index_in_dim(parts, (me - c) % Z, 0, keepdims=False) for c in range(Z)]
+    def shift(x, axis, size, k):
+        return lax.ppermute(x, axis, [(i, (i + k) % size) for i in range(size)])
 
     kv = lax.all_gather(swap(by_head(key_rows, value_rows)), ("y", "core"), axis=0)
     qd = swap(by_head(query_rows, out_grad)).reshape(Z * BLK, -1)
-    dq, keep, give = attention(lists, counts, jnp.stack([core, lax.axis_index("z")]), qd, kv, hot, bias)
-    dq = turn(dq)
-    other = lax.ppermute(give, "core", [(0, 1), (1, 0)])
-    dkv = swap((keep.astype(F32) + other.astype(F32)).astype(BF16), "y")
-    dkv, dq = lax.optimization_barrier((dkv, dq))
-    dkv = swap(jnp.sum(dkv.astype(F32), axis=0).astype(BF16))
-    dq = jnp.concatenate(in_order(dq), axis=1)
+    dq, keep, give = attention(lists, counts, jnp.stack([core, lax.axis_index("y")]), qd, kv, hot, bias)
+    dq = swap(dq)
+    other = shift(give, "core", C, 1)
+    both = [(keep[k].astype(F32) + other[k].astype(F32)).astype(BF16) for k in range(Y)]
+    parts = [both[0]] + [shift(both[k], "y", Y, k) for k in range(1, Y)]
+    parts, dq = lax.optimization_barrier((parts, dq))
+    dkv = functools.reduce(jnp.add, [part.astype(F32) for part in parts]).astype(BF16)
+    dkv = swap(dkv)
+    dq = jnp.concatenate([dq[c] for c in range(Z)], axis=1)
     dk = jnp.concatenate([dkv[c, :, :HEAD] for c in range(Z)], axis=1)
     dv = jnp.concatenate([dkv[c, :, HEAD:] for c in range(Z)], axis=1)
     return dq, dk, dv

time: 185 us -> 189 us (1.022); the launches traced: 184 us -> 185 us
  starting transfers between devices: 38.9 us -> 33.1 us
  waiting for transfers between devices: 44.1 us -> 49.7 us
    all_to_all x3, starting transfers between devices: 28.6 us -> 19.5 us  [swap(): return lax.all_to_all(x, axis, 0, 0, tiled=True)]
    ppermute x4, waiting for transfers between devices: 12.5 us -> 19 us  [shift(): return lax.ppermute(x, axis, [(i, (i + k) % size) for i in range(size)])]
    ppermute x4, starting transfers between devices: 10.2 us -> 13.6 us  [shift(): return lax.ppermute(x, axis, [(i, (i + k) % size) for i in range(size)])]
  transfers between devices with their start and end apart: 8 -> 8, of which waited for: 7 -> 6; matrix products, arithmetic and copies ran while one was open for 4% -> 5% of each run, Pallas kernels for 0% -> 0%
where the time goes in v4:
time: 189 us; the launch traced here: 185 us
  Pallas kernels  52 us (28%)
  waiting for transfers between devices  49.7 us (26%)
  starting transfers between devices  33.1 us (18%)
  blocking collectives  22.3 us (12%)
  between operations  14.2 us (8%)
  other arithmetic  11 us (6%)
  local copies, waits for them, and re-layouts  2.51 us (1%)
    pallas_call x1, Pallas kernels, attention(): pl.pallas_call(attn_kernel, grid_spec=pltpu.PrefetchScalarGridSpec(num_sc...  52 us
    all_to_all x3, waiting for transfers between devices, swap(): return lax.all_to_all(x, axis, 0, 0, tiled=True)  30.4 us
    all_to_all x1, blocking collectives, swap(): return lax.all_to_all(x, axis, 0, 0, tiled=True)  22.3 us
    all_to_all x3, starting transfers between devices, swap(): return lax.all_to_all(x, axis, 0, 0, tiled=True)  19.5 us
    ppermute x4, waiting for transfers between devices, shift(): return lax.ppermute(x, axis, [(i, (i + k) % size) for i in range(size)])  19 us
    ppermute x4, starting transfers between devices, shift(): return lax.ppermute(x, axis, [(i, (i + k) % size) for i in range(size)])  13.6 us
  transfers between devices with their start and end apart: 8, of which 6 were waited for; matrix products, arithmetic and copies ran while one was open for 5% of the time, Pallas kernels for 0%

profile of v4, /device:TPU:2, one launch (start us, length us, event | category | flops | bytes accessed | tf_op | source)
XLA Modules:
  0.0 185.2 jit_solution(716869609066926720)
XLA Ops:
  7.2 0.9 fusion.13
  8.1 0.9 fusion.14
  9.2 22.3 %all_to_all.20 = bf16[4,192,256]{2,1,0:T(8,128)(2,1)} all-to-all(bf16[4,192,256]{2,1,0:T(8,128)(2,1)S(1)} %pad_maximum_fusion.2), channel_id=1, replica_groups=mesh['z'=4,'y'=4,'core'=2,'dp'=8] {'z'}, dimensions={0} | all-to-all | bytes 786432 | tf_op jit(solution)/shard_map/all_to_all | solution.py:231
  31.8 1.2 pad_maximum_fusion
  33.0 3.7 %all-to-all-start = ((bf16[4,192,768]{2,1,0:T(8,128)(2,1)}), bf16[4,192,768]{2,1,0:T(8,128)(2,1)S(1)}, u32[]{:S(2)}, u32[]{:S(2)}) async-start(bf16[4,192,768]{2,1,0:T(8,128)(2,1)} %pad_maximum_fusion), calls=%async_computation | async-start | bytes 2359296 | tf_op jit(solution)/shard_map/all_to_all | solution.py:231
  36.8 0.6 fusion.2
  37.5 0.1 copy.12
  37.6 0.1 eq.60
  37.7 0.3 fusion.15
  38.0 0.1 and_reduce_fusion
  38.1 0.1 convert_reduce_fusion.1.counts
  38.3 0.2 convert_reduce_fusion
  38.4 0.2 select_reduce_fusion
  38.6 0.1 add.51.lists
  38.9 2.5 %fusion.hot_ref = bf16[33,192,128]{2,1,0:T(8,128)(2,1)} fusion(s32[33,192]{1,0:T(8,128)S(1)} %concatenate.44), kind=kLoop, calls=%fused_computation.1 | loop fusion | flops 1622016 | bytes 1647360 | tf_op jit(solution)/shard_map/convert_element_type | solution.py:204
  41.3 17.6 %all-to-all-done = bf16[4,192,768]{2,1,0:T(8,128)(2,1)S(1)} async-done(((bf16[4,192,768]{2,1,0:T(8,128)(2,1)}), bf16[4,192,768]{2,1,0:T(8,128)(2,1)S(1)}, u32[]{:S(2)}, u32[]{:S(2)}) %all-to-all-start) | async-done | bytes 1179680 | tf_op jit(solution)/shard_map/all_to_all | solution.py:231
  58.9 0.3 all-gather.3.cloned.1.call-done
  59.2 52.0 %shard_map.85 = (bf16[4,192,384]{2,1,0:T(8,128)(2,1)}, bf16[4,4,192,256]{3,2,1,0:T(8,128)(2,1)S(1)}, bf16[4,4,192,256]{3,2,1,0:T(8,128)(2,1)}) custom-call(s32[96]{0:T(128)S(1)} %add.51.lists, s32[3]{0:T(128)S(1)} %convert_reduce_fusion.1.counts, s32[2]{0:T(128)S(1)} %pad_add_fusion.spot, bf16[768,768]{1,0:T(8,128)(2,1)S(1)} %bitcast.59, ...), custom_call_target="tpu_custom_call" | custom-call | tf_op jit(solution)/shard_map/pallas_call | solution.py:166
  111.2 8.9 %all-to-all-start.2 = ((bf16[4,192,384]{2,1,0:T(8,128)(2,1)}), bf16[4,192,384]{2,1,0:T(8,128)(2,1)S(1)}, u32[]{:S(2)}, u32[]{:S(2)}) async-start(bf16[4,192,384]{2,1,0:T(8,128)(2,1)} %get-tuple-element.13), calls=%async_computation.2 | async-start | bytes 1179648 | tf_op jit(solution)/shard_map/all_to_all | solution.py:231
  120.1 2.6 %fusion.6 = (bf16[4,192,256]{2,1,0:T(8,128)(2,1)}, bf16[4,192,256]{2,1,0:T(8,128)(2,1)S(1)}, bf16[4,192,256]{2,1,0:T(8,128)(2,1)S(1)}, bf16[4,192,256]{2,1,0:T(8,128)(2,1)S(1)}) fusion(bf16[4,4,192,256]{3,2,1,0:T(8,128)(2,1)} %collective-permute-done, bf16[4,4,192,256]{3,2,1,0:T(8,128)(2,1)S(1)} %get-tuple-element.11), kind=kLoop, calls=%fused_computation.16 | loop fusion | flops 3145728 | bytes 4718592 | tf_op jit(solution)/shard_map/convert_element_type | solution.py:241
  122.6 12.0 %collective-permute-start.3 = (bf16[4,192,256]{2,1,0:T(8,128)(2,1)}, bf16[4,192,256]{2,1,0:T(8,128)(2,1)S(1)}, u32[]{:S(2)}, u32[]{:S(2)}) collective-permute-start(bf16[4,192,256]{2,1,0:T(8,128)(2,1)} %get-tuple-element.19), channel_id=1, source_target_pairs={{0,48},{16,0},{32,16},{48,32},{1,49},{17,1},{33,17},{49,33},{2,50}... | collective-permute-start | bytes 1179656 | tf_op jit(solution)/shard_map/ppermute | solution.py:234
  134.7 0.2 collective-permute-start.2
  134.9 1.4 collective-permute-start.1
  136.3 0.2 all-to-all-done.2
  136.5 15.7 %collective-permute-done.3 = bf16[4,192,256]{2,1,0:T(8,128)(2,1)S(1)} collective-permute-done((bf16[4,192,256]{2,1,0:T(8,128)(2,1)}, bf16[4,192,256]{2,1,0:T(8,128)(2,1)S(1)}, u32[]{:S(2)}, u32[]{:S(2)}) %collective-permute-start.3) | collective-permute-done | bytes 393248 | tf_op jit(solution)/shard_map/ppermute | solution.py:234
  152.2 3.3 %collective-permute-done.1 = bf16[4,192,256]{2,1,0:T(8,128)(2,1)S(1)} collective-permute-done((bf16[4,192,256]{2,1,0:T(8,128)(2,1)S(1)}, bf16[4,192,256]{2,1,0:T(8,128)(2,1)S(1)}, u32[]{:S(2)}, u32[]{:S(2)}) %collective-permute-start.1) | collective-permute-done | bytes 393248 | tf_op jit(solution)/shard_map/ppermute | solution.py:234
  155.5 0.9 add_convert_fusion
  156.4 6.9 %all-to-all-start.3 = ((bf16[4,192,256]{2,1,0:T(8,128)(2,1)}), bf16[4,192,256]{2,1,0:T(8,128)(2,1)S(1)}, u32[]{:S(2)}, u32[]{:S(2)}) async-start(bf16[4,192,256]{2,1,0:T(8,128)(2,1)} %add_convert_fusion), calls=%async_computation.3 | async-start | bytes 786432 | tf_op jit(solution)/shard_map/all_to_all | solution.py:231
  163.4 0.9 pad_maximum_fusion.1
  164.2 12.6 %all-to-all-done.3 = bf16[4,192,256]{2,1,0:T(8,128)(2,1)S(1)} async-done(((bf16[4,192,256]{2,1,0:T(8,128)(2,1)}), bf16[4,192,256]{2,1,0:T(8,128)(2,1)S(1)}, u32[]{:S(2)}, u32[]{:S(2)}) %all-to-all-start.3) | async-done | bytes 393248 | tf_op jit(solution)/shard_map/all_to_all | solution.py:231
  177.0 0.7 pad_maximum_fusion.4
  177.7 0.7 pad_maximum_fusion.3
  (32 shorter events, 0.9 us)
Async XLA Ops:
  7.2 52.0 %all-gather.3.cloned.1.call-start = ((), (), s32[]{:S(2)}) async-start(), calls=%async_computation.4 | async-start | bytes 3538944 | tf_op jit(solution)/shard_map/all_gather | solution.py:236
  9.0 22.5 %copy-start = (bf16[192,1536]{1,0:T(8,128)(2,1)S(1)}, bf16[192,1536]{1,0:T(8,128)(2,1)}, u32[]{:S(2)}) copy-start(bf16[192,1536]{1,0:T(8,128)(2,1)} %param.6) | copy-start | bytes 1769476
  9.1 22.5 %copy-start.1 = (bf16[192,1536]{1,0:T(8,128)(2,1)S(1)}, bf16[192,1536]{1,0:T(8,128)(2,1)}, u32[]{:S(2)}) copy-start(bf16[192,1536]{1,0:T(8,128)(2,1)} %param.9) | copy-start | bytes 1769476
  33.0 3.7 %copy-start.2 = (s32[6144]{0:T(1024)S(1)}, s32[6144]{0:T(1024)}, u32[]{:S(2)}) copy-start(s32[6144]{0:T(1024)} %param.10) | copy-start | bytes 73732
  33.0 4.7 %copy-start.3 = (s32[16,16]{1,0:T(8,128)S(1)}, s32[16,16]{1,0:T(8,128)}, u32[]{:S(2)}) copy-start(s32[16,16]{1,0:T(8,128)} %param.11) | copy-start | bytes 3076
  33.0 25.9 %all-to-all-start = ((bf16[4,192,768]{2,1,0:T(8,128)(2,1)}), bf16[4,192,768]{2,1,0:T(8,128)(2,1)S(1)}, u32[]{:S(2)}, u32[]{:S(2)}) async-start(bf16[4,192,768]{2,1,0:T(8,128)(2,1)} %pad_maximum_fusion), calls=%async_computation | async-start | bytes 2359296 | tf_op jit(solution)/shard_map/all_to_all | solution.py:231
  111.2 8.9 %collective-permute-start = (bf16[4,4,192,256]{3,2,1,0:T(8,128)(2,1)}, bf16[4,4,192,256]{3,2,1,0:T(8,128)(2,1)}, u32[]{:S(2)}, u32[]{:S(2)}) collective-permute-start(bf16[4,4,192,256]{3,2,1,0:T(8,128)(2,1)} %get-tuple-element.12), channel_id=1, source_target_pairs={{0,8},{8,0},{1,9},{9,1},{2,10},{10,2},{3,11},{11,3},{4,12},{12,4},... | collective-permute-start | bytes 4718600 | tf_op jit(solution)/shard_map/ppermute | solution.py:234
  111.2 25.3 %all-to-all-start.2 = ((bf16[4,192,384]{2,1,0:T(8,128)(2,1)}), bf16[4,192,384]{2,1,0:T(8,128)(2,1)S(1)}, u32[]{:S(2)}, u32[]{:S(2)}) async-start(bf16[4,192,384]{2,1,0:T(8,128)(2,1)} %get-tuple-element.13), calls=%async_computation.2 | async-start | bytes 1179648 | tf_op jit(solution)/shard_map/all_to_all | solution.py:231
  122.6 29.5 %collective-permute-start.3 = (bf16[4,192,256]{2,1,0:T(8,128)(2,1)}, bf16[4,192,256]{2,1,0:T(8,128)(2,1)S(1)}, u32[]{:S(2)}, u32[]{:S(2)}) collective-permute-start(bf16[4,192,256]{2,1,0:T(8,128)(2,1)} %get-tuple-element.19), channel_id=1, source_target_pairs={{0,48},{16,0},{32,16},{48,32},{1,49},{17,1},{33,17},{49,33},{2,50}... | collective-permute-start | bytes 1179656 | tf_op jit(solution)/shard_map/ppermute | solution.py:234
  134.7 17.5 %collective-permute-start.2 = (bf16[4,192,256]{2,1,0:T(8,128)(2,1)S(1)}, bf16[4,192,256]{2,1,0:T(8,128)(2,1)S(1)}, u32[]{:S(2)}, u32[]{:S(2)}) collective-permute-start(bf16[4,192,256]{2,1,0:T(8,128)(2,1)S(1)} %get-tuple-element.20), channel_id=1, source_target_pairs={{0,32},{16,48},{32,0},{48,16},{1,33},{17,49},{33,1},{49,17},{2,34}... | collective-permute-start | bytes 1179656 | tf_op jit(solution)/shard_map/ppermute | solution.py:234
  134.9 20.6 %collective-permute-start.1 = (bf16[4,192,256]{2,1,0:T(8,128)(2,1)S(1)}, bf16[4,192,256]{2,1,0:T(8,128)(2,1)S(1)}, u32[]{:S(2)}, u32[]{:S(2)}) collective-permute-start(bf16[4,192,256]{2,1,0:T(8,128)(2,1)S(1)} %get-tuple-element.21), channel_id=1, source_target_pairs={{0,16},{16,32},{32,48},{48,0},{1,17},{17,33},{33,49},{49,1},{2,18}... | collective-permute-start | bytes 1179656 | tf_op jit(solution)/shard_map/ppermute | solution.py:234
  156.4 20.5 %all-to-all-start.3 = ((bf16[4,192,256]{2,1,0:T(8,128)(2,1)}), bf16[4,192,256]{2,1,0:T(8,128)(2,1)S(1)}, u32[]{:S(2)}, u32[]{:S(2)}) async-start(bf16[4,192,256]{2,1,0:T(8,128)(2,1)} %add_convert_fusion), calls=%async_computation.3 | async-start | bytes 786432 | tf_op jit(solution)/shard_map/all_to_all | solution.py:231
Sparse Core Ops, SparseCore 0:
  31.6 27.5 all-gather.2

commit v5 on v4

--- a/solution.py
+++ b/solution.py
@@ -43,14 +43,20 @@
     return op(x.reshape(x.shape[0] // 8, 8, x.shape[1]), axis=0)
 
 
-def attn_kernel(lists, counts, spot, qd_all, kv_ref, hot_ref, bias_ref, dq_ref, keep_ref, give_ref,
-                acc, dpbuf, pbuf, qt, dot_t, qs, dos, stat_m, stat_l, stat_d, dqt):
+def attn_kernel(lists, counts, spot, qd0, qd1, qd2, qd3, kv_ref, hot_ref, bias_ref, dq_ref, keep_ref, give_ref,
+                qd_all, acc, dpbuf, pbuf, qt, dot_t, qs, dos, stat_m, stat_l, stat_d, dqt):
     r = pl.program_id(0)
+
+    def slot(q):
+        return (spot[2] + Z - q) % Z
+
     qd_ref = qd_all.at[pl.ds(pl.multiple_of(r * QT, QT), QT)]
 
     @pl.when(r == 0)
     def _():
         acc[...] = jnp.zeros_like(acc)
+        for k, part in enumerate((qd0, qd1, qd2, qd3)):
+            qd_all[pl.ds(pl.multiple_of(slot(k) * BLK, BLK), BLK)] = part[...]
 
     for h in range(GROUP):
         q = qd_ref[:, h * HEAD:(h + 1) * HEAD]
@@ -64,7 +70,7 @@
     def blocks(i):
         ids = [lists[r * NB + i * WIDE + j] for j in range(WIDE)]
         real = [jnp.minimum(b, NB - 1) for b in ids]
-        return ids, [(b % T, b // T) for b in real]
+        return ids, [(b % T, slot(b // T)) for b in real]
 
     def masked_keys(ids, where):
         return jnp.concatenate(
@@ -150,7 +156,7 @@
                 while row < QT:
                     q, start = divmod(tile * QT + row, BLK)
                     take = min(BLK - start, QT - row)
-                    dq_ref[q, start:start + take, h * HEAD:(h + 1) * HEAD] = dq[row:row + take]
+                    dq_ref[slot(q), start:start + take, h * HEAD:(h + 1) * HEAD] = dq[row:row + take]
                     row += take
 
     @pl.when(r == NQ - 1)
@@ -161,16 +167,17 @@
             give_ref[i] = acc[y * C + 1 - spot[0]].astype(BF16)
 
 
-def attention(lists, counts, spot, qd, kv, hot, bias):
+def attention(lists, counts, spot, qd_parts, kv, hot, bias):
     vmem = pl.BlockSpec(memory_space=pltpu.VMEM)
     return pl.pallas_call(
         attn_kernel,
         grid_spec=pltpu.PrefetchScalarGridSpec(
             num_scalar_prefetch=3,
             grid=(NQ,),
-            in_specs=[vmem] * 4,
+            in_specs=[vmem] * (Z + 3),
             out_specs=[vmem] * 3,
             scratch_shapes=[
+                pltpu.VMEM((Z * BLK, 2 * GROUP * HEAD), BF16),
                 pltpu.VMEM((T, Z, BLK, 2 * HEAD), F32),
                 pltpu.VMEM((NI, KT, GROUP * QT), F32),
                 pltpu.VMEM((NI, KT, GROUP * QT), BF16),
@@ -192,7 +199,7 @@
         compiler_params=pltpu.CompilerParams(
             dimension_semantics=("arbitrary",), vmem_limit_bytes=LIMIT * 1024 * 1024
         ),
-    )(lists, counts, spot, qd, kv, hot, bias)
+    )(lists, counts, spot, *qd_parts, kv, hot, bias)
 
 
 def masks(token_span, visible, t_index):
@@ -223,30 +230,39 @@
     core = lax.axis_index("core")
     hot, bias, lists, counts = masks(token_span, visible, lax.axis_index("y") * C + core)
 
-    def by_head(x, y):
-        m, n = x.shape[1] // Z, y.shape[1] // Z
-        return jnp.stack([jnp.concatenate([x[:, c * m:(c + 1) * m], y[:, c * n:(c + 1) * n]], axis=1) for c in range(Z)])
-
-    def swap(x, axis="z"):
-        return lax.all_to_all(x, axis, 0, 0, tiled=True)
+    me = lax.axis_index("z")
 
     def shift(x, axis, size, k):
         return lax.ppermute(x, axis, [(i, (i + k) % size) for i in range(size)])
 
-    kv = lax.all_gather(swap(by_head(key_rows, value_rows)), ("y", "core"), axis=0)
-    qd = swap(by_head(query_rows, out_grad)).reshape(Z * BLK, -1)
-    dq, keep, give = attention(lists, counts, jnp.stack([core, lax.axis_index("y")]), qd, kv, hot, bias)
-    dq = swap(dq)
+    def for_head(x, y, c):
+        m, n = x.shape[1] // Z, y.shape[1] // Z
+        return jnp.concatenate(
+            [lax.dynamic_slice_in_dim(x, c * m, m, 1), lax.dynamic_slice_in_dim(y, c * n, n, 1)], axis=1)
+
+    def send(parts, sign):
+        return [parts[0]] + [shift(parts[k], "z", Z, sign * k) for k in range(1, Z)]
+
+    def in_order(parts, lo, hi):
+        parts = jnp.stack(parts)
+        return jnp.concatenate(
+            [lax.dynamic_index_in_dim(parts, (c + Z - me) % Z, 0, keepdims=False)[:, lo:hi] for c in range(Z)], axis=1)
+
+    kv = send([for_head(key_rows, value_rows, (me + k) % Z) for k in range(Z)], 1)
+    qd = [for_head(query_rows, out_grad, (me + k) % Z) for k in range(Z)]
+    kv, qd, hot, bias, lists, counts = lax.optimization_barrier((kv, qd, hot, bias, lists, counts))
+    kv = lax.all_gather(jnp.stack(kv), ("y", "core"), axis=0)
+    qd = send(qd, 1)
+    spot = jnp.stack([core, lax.axis_index("y"), me])
+    dq, keep, give = attention(lists, counts, spot, qd, kv, hot, bias)
+    dq = send([dq[k] for k in range(Z)], -1)
     other = shift(give, "core", C, 1)
     both = [(keep[k].astype(F32) + other[k].astype(F32)).astype(BF16) for k in range(Y)]
     parts = [both[0]] + [shift(both[k], "y", Y, k) for k in range(1, Y)]
     parts, dq = lax.optimization_barrier((parts, dq))
     dkv = functools.reduce(jnp.add, [part.astype(F32) for part in parts]).astype(BF16)
-    dkv = swap(dkv)
-    dq = jnp.concatenate([dq[c] for c in range(Z)], axis=1)
-    dk = jnp.concatenate([dkv[c, :, :HEAD] for c in range(Z)], axis=1)
-    dv = jnp.concatenate([dkv[c, :, HEAD:] for c in range(Z)], axis=1)
-    return dq, dk, dv
+    dkv = send([dkv[k] for k in range(Z)], -1)
+    return in_order(dq, 0, GROUP * HEAD), in_order(dkv, 0, HEAD), in_order(dkv, HEAD, 2 * HEAD)
 
 
 def solution(mesh):

time: 189 us -> 178 us (0.942); the launches traced: 185 us -> 180 us
  blocking collectives: 22.3 us -> 0 us
  starting transfers between devices: 33.1 us -> 42.5 us
  waiting for transfers between devices: 49.7 us -> 55.1 us
  Pallas kernels: 52 us -> 56.7 us
  other arithmetic: 11 us -> 8.03 us
    ppermute x4 -> x16, waiting for transfers between devices: 19 us -> 55.1 us  [shift(): return lax.ppermute(x, axis, [(i, (i + k) % size) for i in range(size)])]
    all_to_all x3 -> x0, waiting for transfers between devices: 30.4 us -> none  [swap(): return lax.all_to_all(x, axis, 0, 0, tiled=True)]
    ppermute x4 -> x16, starting transfers between devices: 13.6 us -> 42.5 us  [shift(): return lax.ppermute(x, axis, [(i, (i + k) % size) for i in range(size)])]
    all_to_all x1 -> x0, blocking collectives: 22.3 us -> none  [swap(): return lax.all_to_all(x, axis, 0, 0, tiled=True)]
    all_to_all x3 -> x0, starting transfers between devices: 19.5 us -> none  [swap(): return lax.all_to_all(x, axis, 0, 0, tiled=True)]
    pallas_call x1, Pallas kernels: 52 us -> 56.7 us  [attention(): pl.pallas_call(attn_kernel, grid_spec=pltpu.PrefetchScalarGridSpec(num_sc...]
    convert_element_type x1, other arithmetic: 2.55 us -> 0.49 us  [per_device(): (keep[k].astype(F32) + other[k].astype(F32)).astype(BF16)]
  transfers between devices with their start and end apart: 8 -> 17, of which waited for: 6 -> 11; matrix products, arithmetic and copies ran while one was open for 5% -> 4% of each run, Pallas kernels for 0% -> 0%
where the time goes in v5:
time: 178 us; the launch traced here: 180 us
  Pallas kernels  56.7 us (32%)
  waiting for transfers between devices  55.1 us (31%)
  starting transfers between devices  42.5 us (24%)
  between operations  14.3 us (8%)
  other arithmetic  8.03 us (5%)
  local copies, waits for them, and re-layouts  3.33 us (2%)
    pallas_call x1, Pallas kernels, attention(): pl.pallas_call(attn_kernel, grid_spec=pltpu.PrefetchScalarGridSpec(num_sc...  56.7 us
    ppermute x16, waiting for transfers between devices, shift(): return lax.ppermute(x, axis, [(i, (i + k) % size) for i in range(size)])  55.1 us
    ppermute x16, starting transfers between devices, shift(): return lax.ppermute(x, axis, [(i, (i + k) % size) for i in range(size)])  42.5 us
  transfers between devices with their start and end apart: 17, of which 11 were waited for; matrix products, arithmetic and copies ran while one was open for 4% of the time, Pallas kernels for 0%

profile of v5, /device:TPU:2, one launch (start us, length us, event | category | flops | bytes accessed | tf_op | source)
XLA Modules:
  0.0 180.2 jit_solution(8689583266652680608)
XLA Ops:
  7.3 1.1 constant_dynamic-slice_fusion.9
  8.4 6.4 %collective-permute-start.2 = (bf16[192,256]{1,0:T(8,128)(2,1)S(1)}, bf16[192,256]{1,0:T(8,128)(2,1)S(1)}, u32[]{:S(2)}, u32[]{:S(2)}) collective-permute-start(bf16[192,256]{1,0:T(8,128)(2,1)S(1)} %pad_maximum_fusion.13), channel_id=1, source_target_pairs={{0,192},{64,0},{128,64},{192,128},{1,193},{65,1},{129,65},{193,129... | collective-permute-start | bytes 294920 | tf_op jit(solution)/shard_map/ppermute | solution.py:236
  14.8 1.0 collective-permute-start.1
  15.9 3.0 %collective-permute-start = (bf16[192,256]{1,0:T(8,128)(2,1)S(1)}, bf16[192,256]{1,0:T(8,128)(2,1)S(1)}, u32[]{:S(2)}, u32[]{:S(2)}) collective-permute-start(bf16[192,256]{1,0:T(8,128)(2,1)S(1)} %pad_maximum_fusion.11), channel_id=1, source_target_pairs={{0,64},{64,128},{128,192},{192,0},{1,65},{65,129},{129,193},{193,1... | collective-permute-start | bytes 294920 | tf_op jit(solution)/shard_map/ppermute | solution.py:236
  18.8 0.8 reshape.61
  21.6 2.5 %fusion.hot_ref = bf16[33,192,128]{2,1,0:T(8,128)(2,1)} fusion(s32[33,192]{1,0:T(8,128)S(1)} %concatenate.44), kind=kLoop, calls=%fused_computation.1 | loop fusion | flops 1622016 | bytes 1647360 | tf_op jit(solution)/shard_map/convert_element_type | solution.py:211
  24.5 1.9 %collective-permute-done.1 = bf16[192,256]{1,0:T(8,128)(2,1)S(1)} collective-permute-done((bf16[192,256]{1,0:T(8,128)(2,1)S(1)}, bf16[192,256]{1,0:T(8,128)(2,1)S(1)}, u32[]{:S(2)}, u32[]{:S(2)}) %collective-permute-start.1) | collective-permute-done | bytes 98336 | tf_op jit(solution)/shard_map/ppermute | solution.py:236
  26.4 0.8 pad_maximum_fusion.2
  27.2 0.9 collective-permute-start.3
  28.1 4.1 %collective-permute-start.4 = (bf16[192,768]{1,0:T(8,128)(2,1)S(1)}, bf16[192,768]{1,0:T(8,128)(2,1)S(1)}, u32[]{:S(2)}, u32[]{:S(2)}) collective-permute-start(bf16[192,768]{1,0:T(8,128)(2,1)S(1)} %pad_maximum_fusion.6), channel_id=1, source_target_pairs={{0,128},{64,192},{128,0},{192,64},{1,129},{65,193},{129,1},{193,65... | collective-permute-start | bytes 884744 | tf_op jit(solution)/shard_map/ppermute | solution.py:236
  32.1 4.0 %collective-permute-start.5 = (bf16[192,768]{1,0:T(8,128)(2,1)S(1)}, bf16[192,768]{1,0:T(8,128)(2,1)S(1)}, u32[]{:S(2)}, u32[]{:S(2)}) collective-permute-start(bf16[192,768]{1,0:T(8,128)(2,1)S(1)} %pad_maximum_fusion.7), channel_id=1, source_target_pairs={{0,192},{64,0},{128,64},{192,128},{1,193},{65,1},{129,65},{193,129... | collective-permute-start | bytes 884744 | tf_op jit(solution)/shard_map/ppermute | solution.py:236
  36.3 4.6 %collective-permute-done.3.qd1 = bf16[192,768]{1,0:T(8,128)(2,1)S(1)} collective-permute-done((bf16[192,768]{1,0:T(8,128)(2,1)S(1)}, bf16[192,768]{1,0:T(8,128)(2,1)S(1)}, u32[]{:S(2)}, u32[]{:S(2)}) %collective-permute-start.3) | collective-permute-done | bytes 294944 | tf_op jit(solution)/shard_map/ppermute | solution.py:236
  40.9 6.2 %collective-permute-done.4.qd2 = bf16[192,768]{1,0:T(8,128)(2,1)S(1)} collective-permute-done((bf16[192,768]{1,0:T(8,128)(2,1)S(1)}, bf16[192,768]{1,0:T(8,128)(2,1)S(1)}, u32[]{:S(2)}, u32[]{:S(2)}) %collective-permute-start.4) | collective-permute-done | bytes 294944 | tf_op jit(solution)/shard_map/ppermute | solution.py:236
  47.0 11.6 %collective-permute-done.5.qd3 = bf16[192,768]{1,0:T(8,128)(2,1)S(1)} collective-permute-done((bf16[192,768]{1,0:T(8,128)(2,1)S(1)}, bf16[192,768]{1,0:T(8,128)(2,1)S(1)}, u32[]{:S(2)}, u32[]{:S(2)}) %collective-permute-start.5) | collective-permute-done | bytes 294944 | tf_op jit(solution)/shard_map/ppermute | solution.py:236
  58.6 56.7 %shard_map.85 = (bf16[4,192,384]{2,1,0:T(8,128)(2,1)S(1)}, bf16[4,4,192,256]{3,2,1,0:T(8,128)(2,1)S(1)}, bf16[4,4,192,256]{3,2,1,0:T(8,128)(2,1)S(1)}) custom-call(s32[96]{0:T(128)S(1)} %add.169.lists, s32[3]{0:T(128)S(1)} %convert_reduce_fusion.1.counts, s32[3]{0:T(128)S(1)} %pad_add_fusion.spot, bf16[192,768]{1,0:T(8,128)(2,1)S(1)} %pad_maximum_fusion.4.qd0, ...), custom_call_target="tpu_custom_call" | custom-call | tf_op jit(solution)/shard_map/pallas_call | solution.py:172
  115.4 3.4 %collective-permute-done.6 = bf16[4,4,192,256]{3,2,1,0:T(8,128)(2,1)S(1)} collective-permute-done((bf16[4,4,192,256]{3,2,1,0:T(8,128)(2,1)S(1)}, bf16[4,4,192,256]{3,2,1,0:T(8,128)(2,1)S(1)}, u32[]{:S(2)}, u32[]{:S(2)}) %collective-permute-start.6) | collective-permute-done | bytes 1572896 | tf_op jit(solution)/shard_map/ppermute | solution.py:236
  119.3 3.2 %collective-permute-start.7 = (bf16[4,192,256]{2,1,0:T(8,128)(2,1)S(1)}, bf16[4,192,256]{2,1,0:T(8,128)(2,1)S(1)}, u32[]{:S(2)}, u32[]{:S(2)}) collective-permute-start(bf16[4,192,256]{2,1,0:T(8,128)(2,1)S(1)} %get-tuple-element.51), channel_id=1, source_target_pairs={{0,16},{16,32},{32,48},{48,0},{1,17},{17,33},{33,49},{49,1},{2,18}... | collective-permute-start | bytes 1179656 | tf_op jit(solution)/shard_map/ppermute | solution.py:236
  122.5 10.5 %collective-permute-start.8 = (bf16[4,192,256]{2,1,0:T(8,128)(2,1)S(1)}, bf16[4,192,256]{2,1,0:T(8,128)(2,1)S(1)}, u32[]{:S(2)}, u32[]{:S(2)}) collective-permute-start(bf16[4,192,256]{2,1,0:T(8,128)(2,1)S(1)} %get-tuple-element.50), channel_id=1, source_target_pairs={{0,32},{16,48},{32,0},{48,16},{1,33},{17,49},{33,1},{49,17},{2,34}... | collective-permute-start | bytes 1179656 | tf_op jit(solution)/shard_map/ppermute | solution.py:236
  133.0 0.7 slice_bitcast_fusion
  133.7 4.6 %collective-permute-start.10 = (bf16[192,384]{1,0:T(8,128)(2,1)S(1)}, bf16[192,384]{1,0:T(8,128)(2,1)S(1)}, u32[]{:S(2)}, u32[]{:S(2)}) collective-permute-start(bf16[192,384]{1,0:T(8,128)(2,1)S(1)} %get-tuple-element.59), channel_id=1, source_target_pairs={{0,192},{64,0},{128,64},{192,128},{1,193},{65,1},{129,65},{193,129... | collective-permute-start | bytes 442376 | tf_op jit(solution)/shard_map/ppermute | solution.py:236
  138.3 0.9 collective-permute-start.11
  139.2 8.6 %collective-permute-done.10 = bf16[192,384]{1,0:T(8,128)(2,1)S(1)} collective-permute-done((bf16[192,384]{1,0:T(8,128)(2,1)S(1)}, bf16[192,384]{1,0:T(8,128)(2,1)S(1)}, u32[]{:S(2)}, u32[]{:S(2)}) %collective-permute-start.10) | collective-permute-done | bytes 147488 | tf_op jit(solution)/shard_map/ppermute | solution.py:236
  147.8 4.9 %collective-permute-done.11 = bf16[192,384]{1,0:T(8,128)(2,1)S(1)} collective-permute-done((bf16[192,384]{1,0:T(8,128)(2,1)}, bf16[192,384]{1,0:T(8,128)(2,1)S(1)}, u32[]{:S(2)}, u32[]{:S(2)}) %collective-permute-start.11) | collective-permute-done | bytes 147488 | tf_op jit(solution)/shard_map/ppermute | solution.py:236
  152.7 4.7 %collective-permute-done.12 = bf16[192,384]{1,0:T(8,128)(2,1)S(1)} collective-permute-done((bf16[192,384]{1,0:T(8,128)(2,1)S(1)}, bf16[192,384]{1,0:T(8,128)(2,1)S(1)}, u32[]{:S(2)}, u32[]{:S(2)}) %collective-permute-start.12) | collective-permute-done | bytes 147488 | tf_op jit(solution)/shard_map/ppermute | solution.py:236
  157.7 1.4 collective-permute-start.13
  159.1 2.5 %collective-permute-start.15 = (bf16[192,256]{1,0:T(8,128)(2,1)S(1)}, bf16[192,256]{1,0:T(8,128)(2,1)S(1)}, u32[]{:S(2)}, u32[]{:S(2)}) collective-permute-start(bf16[192,256]{1,0:T(8,128)(2,1)S(1)} %get-tuple-element.74), channel_id=1, source_target_pairs={{0,64},{64,128},{128,192},{192,0},{1,65},{65,129},{129,193},{193,1... | collective-permute-start | bytes 294920 | tf_op jit(solution)/shard_map/ppermute | solution.py:236
  161.7 0.9 pad_maximum_fusion.1
  162.6 3.9 %collective-permute-done.13 = bf16[192,256]{1,0:T(8,128)(2,1)S(1)} collective-permute-done((bf16[192,256]{1,0:T(8,128)(2,1)S(1)}, bf16[192,256]{1,0:T(8,128)(2,1)S(1)}, u32[]{:S(2)}, u32[]{:S(2)}) %collective-permute-start.13) | collective-permute-done | bytes 98336 | tf_op jit(solution)/shard_map/ppermute | solution.py:236
  166.4 4.4 %collective-permute-done.14 = bf16[192,256]{1,0:T(8,128)(2,1)S(1)} collective-permute-done((bf16[192,256]{1,0:T(8,128)(2,1)S(1)}, bf16[192,256]{1,0:T(8,128)(2,1)S(1)}, u32[]{:S(2)}, u32[]{:S(2)}) %collective-permute-start.14) | collective-permute-done | bytes 98336 | tf_op jit(solution)/shard_map/ppermute | solution.py:236
  170.8 0.9 collective-permute-done.15
  171.9 0.7 pad_maximum_fusion.9
  172.6 0.7 pad_maximum_fusion.8
  (58 shorter events, 3.5 us)
Async XLA Ops:
  7.2 12.5 %copy-start.2 = (s32[6144]{0:T(1024)S(1)}, s32[6144]{0:T(1024)}, u32[]{:S(2)}) copy-start(s32[6144]{0:T(1024)} %param.10) | copy-start | bytes 73732
  7.2 13.4 %copy-start.3 = (s32[16,16]{1,0:T(8,128)S(1)}, s32[16,16]{1,0:T(8,128)}, u32[]{:S(2)}) copy-start(s32[16,16]{1,0:T(8,128)} %param.11) | copy-start | bytes 3076
  7.2 51.4 %all-gather.3.cloned.1.call-start = ((), (), s32[]{:S(2)}) async-start(), calls=%async_computation | async-start | bytes 3538944 | tf_op jit(solution)/shard_map/all_gather | solution.py:254
  7.3 16.8 %copy-start = (bf16[192,1536]{1,0:T(8,128)(2,1)S(1)}, bf16[192,1536]{1,0:T(8,128)(2,1)}, u32[]{:S(2)}) copy-start(bf16[192,1536]{1,0:T(8,128)(2,1)} %param.9) | copy-start | bytes 1769476
  7.3 16.8 %copy-start.1 = (bf16[192,1536]{1,0:T(8,128)(2,1)S(1)}, bf16[192,1536]{1,0:T(8,128)(2,1)}, u32[]{:S(2)}) copy-start(bf16[192,1536]{1,0:T(8,128)(2,1)} %param.6) | copy-start | bytes 1769476
  8.4 16.0 %collective-permute-start.2 = (bf16[192,256]{1,0:T(8,128)(2,1)S(1)}, bf16[192,256]{1,0:T(8,128)(2,1)S(1)}, u32[]{:S(2)}, u32[]{:S(2)}) collective-permute-start(bf16[192,256]{1,0:T(8,128)(2,1)S(1)} %pad_maximum_fusion.13), channel_id=1, source_target_pairs={{0,192},{64,0},{128,64},{192,128},{1,193},{65,1},{129,65},{193,129... | collective-permute-start | bytes 294920 | tf_op jit(solution)/shard_map/ppermute | solution.py:236
  14.8 11.5 %collective-permute-start.1 = (bf16[192,256]{1,0:T(8,128)(2,1)S(1)}, bf16[192,256]{1,0:T(8,128)(2,1)S(1)}, u32[]{:S(2)}, u32[]{:S(2)}) collective-permute-start(bf16[192,256]{1,0:T(8,128)(2,1)S(1)} %pad_maximum_fusion.12), channel_id=1, source_target_pairs={{0,128},{64,192},{128,0},{192,64},{1,129},{65,193},{129,1},{193,65... | collective-permute-start | bytes 294920 | tf_op jit(solution)/shard_map/ppermute | solution.py:236
  15.9 10.5 %collective-permute-start = (bf16[192,256]{1,0:T(8,128)(2,1)S(1)}, bf16[192,256]{1,0:T(8,128)(2,1)S(1)}, u32[]{:S(2)}, u32[]{:S(2)}) collective-permute-start(bf16[192,256]{1,0:T(8,128)(2,1)S(1)} %pad_maximum_fusion.11), channel_id=1, source_target_pairs={{0,64},{64,128},{128,192},{192,0},{1,65},{65,129},{129,193},{193,1... | collective-permute-start | bytes 294920 | tf_op jit(solution)/shard_map/ppermute | solution.py:236
  27.2 13.7 %collective-permute-start.3 = (bf16[192,768]{1,0:T(8,128)(2,1)S(1)}, bf16[192,768]{1,0:T(8,128)(2,1)S(1)}, u32[]{:S(2)}, u32[]{:S(2)}) collective-permute-start(bf16[192,768]{1,0:T(8,128)(2,1)S(1)} %pad_maximum_fusion.5), channel_id=1, source_target_pairs={{0,64},{64,128},{128,192},{192,0},{1,65},{65,129},{129,193},{193,1... | collective-permute-start | bytes 884744 | tf_op jit(solution)/shard_map/ppermute | solution.py:236
  28.1 18.9 %collective-permute-start.4 = (bf16[192,768]{1,0:T(8,128)(2,1)S(1)}, bf16[192,768]{1,0:T(8,128)(2,1)S(1)}, u32[]{:S(2)}, u32[]{:S(2)}) collective-permute-start(bf16[192,768]{1,0:T(8,128)(2,1)S(1)} %pad_maximum_fusion.6), channel_id=1, source_target_pairs={{0,128},{64,192},{128,0},{192,64},{1,129},{65,193},{129,1},{193,65... | collective-permute-start | bytes 884744 | tf_op jit(solution)/shard_map/ppermute | solution.py:236
  32.1 26.5 %collective-permute-start.5 = (bf16[192,768]{1,0:T(8,128)(2,1)S(1)}, bf16[192,768]{1,0:T(8,128)(2,1)S(1)}, u32[]{:S(2)}, u32[]{:S(2)}) collective-permute-start(bf16[192,768]{1,0:T(8,128)(2,1)S(1)} %pad_maximum_fusion.7), channel_id=1, source_target_pairs={{0,192},{64,0},{128,64},{192,128},{1,193},{65,1},{129,65},{193,129... | collective-permute-start | bytes 884744 | tf_op jit(solution)/shard_map/ppermute | solution.py:236
  115.3 3.5 %collective-permute-start.6 = (bf16[4,4,192,256]{3,2,1,0:T(8,128)(2,1)S(1)}, bf16[4,4,192,256]{3,2,1,0:T(8,128)(2,1)S(1)}, u32[]{:S(2)}, u32[]{:S(2)}) collective-permute-start(bf16[4,4,192,256]{3,2,1,0:T(8,128)(2,1)S(1)} %get-tuple-element.39), channel_id=1, source_target_pairs={{0,8},{8,0},{1,9},{9,1},{2,10},{10,2},{3,11},{11,3},{4,12},{12,4},... | collective-permute-start | bytes 4718600 | tf_op jit(solution)/shard_map/ppermute | solution.py:236
  119.3 38.2 %collective-permute-start.7 = (bf16[4,192,256]{2,1,0:T(8,128)(2,1)S(1)}, bf16[4,192,256]{2,1,0:T(8,128)(2,1)S(1)}, u32[]{:S(2)}, u32[]{:S(2)}) collective-permute-start(bf16[4,192,256]{2,1,0:T(8,128)(2,1)S(1)} %get-tuple-element.51), channel_id=1, source_target_pairs={{0,16},{16,32},{32,48},{48,0},{1,17},{17,33},{33,49},{49,1},{2,18}... | collective-permute-start | bytes 1179656 | tf_op jit(solution)/shard_map/ppermute | solution.py:236
  122.5 35.0 %collective-permute-start.8 = (bf16[4,192,256]{2,1,0:T(8,128)(2,1)S(1)}, bf16[4,192,256]{2,1,0:T(8,128)(2,1)S(1)}, u32[]{:S(2)}, u32[]{:S(2)}) collective-permute-start(bf16[4,192,256]{2,1,0:T(8,128)(2,1)S(1)} %get-tuple-element.50), channel_id=1, source_target_pairs={{0,32},{16,48},{32,0},{48,16},{1,33},{17,49},{33,1},{49,17},{2,34}... | collective-permute-start | bytes 1179656 | tf_op jit(solution)/shard_map/ppermute | solution.py:236
  133.0 24.4 %collective-permute-start.9 = (bf16[4,192,256]{2,1,0:T(8,128)(2,1)S(1)}, bf16[4,192,256]{2,1,0:T(8,128)(2,1)S(1)}, u32[]{:S(2)}, u32[]{:S(2)}) collective-permute-start(bf16[4,192,256]{2,1,0:T(8,128)(2,1)S(1)} %get-tuple-element.49), channel_id=1, source_target_pairs={{0,48},{16,0},{32,16},{48,32},{1,49},{17,1},{33,17},{49,33},{2,50}... | collective-permute-start | bytes 1179656 | tf_op jit(solution)/shard_map/ppermute | solution.py:236
  133.7 14.1 %collective-permute-start.10 = (bf16[192,384]{1,0:T(8,128)(2,1)S(1)}, bf16[192,384]{1,0:T(8,128)(2,1)S(1)}, u32[]{:S(2)}, u32[]{:S(2)}) collective-permute-start(bf16[192,384]{1,0:T(8,128)(2,1)S(1)} %get-tuple-element.59), channel_id=1, source_target_pairs={{0,192},{64,0},{128,64},{192,128},{1,193},{65,1},{129,65},{193,129... | collective-permute-start | bytes 442376 | tf_op jit(solution)/shard_map/ppermute | solution.py:236
  138.3 14.4 %collective-permute-start.11 = (bf16[192,384]{1,0:T(8,128)(2,1)}, bf16[192,384]{1,0:T(8,128)(2,1)S(1)}, u32[]{:S(2)}, u32[]{:S(2)}) collective-permute-start(bf16[192,384]{1,0:T(8,128)(2,1)} %get-tuple-element.58), channel_id=1, source_target_pairs={{0,128},{64,192},{128,0},{192,64},{1,129},{65,193},{129,1},{193,65... | collective-permute-start | bytes 442376 | tf_op jit(solution)/shard_map/ppermute | solution.py:236
  147.8 9.6 %collective-permute-start.12 = (bf16[192,384]{1,0:T(8,128)(2,1)S(1)}, bf16[192,384]{1,0:T(8,128)(2,1)S(1)}, u32[]{:S(2)}, u32[]{:S(2)}) collective-permute-start(bf16[192,384]{1,0:T(8,128)(2,1)S(1)} %get-tuple-element.57), channel_id=1, source_target_pairs={{0,64},{64,128},{128,192},{192,0},{1,65},{65,129},{129,193},{193,1... | collective-permute-start | bytes 442376 | tf_op jit(solution)/shard_map/ppermute | solution.py:236
  157.7 8.8 %collective-permute-start.13 = (bf16[192,256]{1,0:T(8,128)(2,1)S(1)}, bf16[192,256]{1,0:T(8,128)(2,1)S(1)}, u32[]{:S(2)}, u32[]{:S(2)}) collective-permute-start(bf16[192,256]{1,0:T(8,128)(2,1)S(1)} %get-tuple-element.76), channel_id=1, source_target_pairs={{0,192},{64,0},{128,64},{192,128},{1,193},{65,1},{129,65},{193,129... | collective-permute-start | bytes 294920 | tf_op jit(solution)/shard_map/ppermute | solution.py:236
  159.1 11.8 %collective-permute-start.14 = (bf16[192,256]{1,0:T(8,128)(2,1)S(1)}, bf16[192,256]{1,0:T(8,128)(2,1)S(1)}, u32[]{:S(2)}, u32[]{:S(2)}) collective-permute-start(bf16[192,256]{1,0:T(8,128)(2,1)S(1)} %get-tuple-element.75), channel_id=1, source_target_pairs={{0,128},{64,192},{128,0},{192,64},{1,129},{65,193},{129,1},{193,65... | collective-permute-start | bytes 294920 | tf_op jit(solution)/shard_map/ppermute | solution.py:236
  159.1 12.7 %collective-permute-start.15 = (bf16[192,256]{1,0:T(8,128)(2,1)S(1)}, bf16[192,256]{1,0:T(8,128)(2,1)S(1)}, u32[]{:S(2)}, u32[]{:S(2)}) collective-permute-start(bf16[192,256]{1,0:T(8,128)(2,1)S(1)} %get-tuple-element.74), channel_id=1, source_target_pairs={{0,64},{64,128},{128,192},{192,0},{1,65},{65,129},{129,193},{193,1... | collective-permute-start | bytes 294920 | tf_op jit(solution)/shard_map/ppermute | solution.py:236
Sparse Core Ops, SparseCore 0:
  27.3 30.8 all-gather.2

commit v6 on v5

--- a/solution.py
+++ b/solution.py
@@ -24,7 +24,8 @@
 QT = 256
 NQ = Z * BLK // QT
 NB = Z * T
-WIDE = 4
+WIDE = 8
+HALF = WIDE // 2
 NI = NB // WIDE
 KT = WIDE * BLK
 F32 = jnp.float32
@@ -44,7 +45,7 @@
 
 
 def attn_kernel(lists, counts, spot, qd0, qd1, qd2, qd3, kv_ref, hot_ref, bias_ref, dq_ref, keep_ref, give_ref,
-                qd_all, acc, dpbuf, pbuf, qt, dot_t, qs, dos, stat_m, stat_l, stat_d, dqt):
+                qd_all, acc, dpbuf, pbuf, qt, dot_t, qs, dos, stat_m, stat_l, stat_d, stat_c, dqt):
     r = pl.program_id(0)
 
     def slot(q):
@@ -65,10 +66,11 @@
         qt[h, HEAD:, :] = bias_ref[r]
         dot_t[h] = g.T
     dqt[...] = jnp.zeros_like(dqt)
-    steps = (counts[r] + WIDE - 1) // WIDE
-
-    def blocks(i):
-        ids = [lists[r * NB + i * WIDE + j] for j in range(WIDE)]
+    steps = (counts[r] + HALF - 1) // WIDE
+    odd = counts[r] > steps * WIDE
+
+    def blocks(i, wide):
+        ids = [lists[r * NB + i * WIDE + j] for j in range(wide)]
         real = [jnp.minimum(b, NB - 1) for b in ids]
         return ids, [(b % T, slot(b // T)) for b in real]
 
@@ -77,24 +79,39 @@
             [jnp.concatenate([kv_ref[t, zq, :, :HEAD], hot_ref[b]], axis=1) for b, (t, zq) in zip(ids, where)],
             axis=0)
 
-    def forward(i, carry):
-        ids, where = blocks(i)
+    def every(body):
+        def full(i, carry):
+            body(i, WIDE)
+            return carry
+
+        lax.fori_loop(0, steps, full, 0)
+
+        @pl.when(odd)
+        def _():
+            body(steps, HALF)
+
+    def forward(i, wide):
+        ids, where = blocks(i, wide)
         lhs = masked_keys(ids, where)
         v = jnp.concatenate([kv_ref[t, zq, :, HEAD:] for t, zq in where], axis=0)
         for h in range(GROUP):
             cols = slice(h * QT, (h + 1) * QT)
             p = jnp.exp2(dot(lhs, qt[h]) * (SCALE * LOG2E))
-            dp = dot(v, dot_t[h])
+            dp = dot(v, dot_t[h]) - stat_c[h, :1]
             stat_l[h] += fold(p, jnp.sum)
             stat_d[h] += fold(p * dp, jnp.sum)
-            pbuf[i, :, cols] = p.astype(BF16)
-            dpbuf[i, :, cols] = dp
-        return carry
+            pbuf[i, :wide * BLK, cols] = p.astype(BF16)
+            dpbuf[i, :wide * BLK, cols] = dp.astype(BF16)
+
+    _, ((t0, z0),) = blocks(0, 1)
+    for h in range(GROUP):
+        mean = jnp.sum(dot(kv_ref[t0, z0, :, HEAD:], dot_t[h]), axis=0, keepdims=True) * (1.0 / BLK)
+        stat_c[h] = jnp.broadcast_to(mean, (8, QT))
 
     def forward_all():
         stat_l[...] = jnp.zeros_like(stat_l)
         stat_d[...] = jnp.zeros_like(stat_d)
-        lax.fori_loop(0, steps, forward, 0)
+        every(forward)
         return [jnp.sum(stat_l[h], axis=0, keepdims=True) for h in range(GROUP)]
 
     sums = forward_all()
@@ -105,13 +122,12 @@
     def _():
         stat_m[...] = jnp.full_like(stat_m, NEG)
 
-        def tops(i, carry):
-            lhs = masked_keys(*blocks(i))
+        def tops(i, wide):
+            lhs = masked_keys(*blocks(i, wide))
             for h in range(GROUP):
                 stat_m[h] = jnp.maximum(stat_m[h], fold(dot(lhs, qt[h]), jnp.max))
-            return carry
-
-        lax.fori_loop(0, steps, tops, 0)
+
+        every(tops)
         for h in range(GROUP):
             top = jnp.max(stat_m[h], axis=0, keepdims=True)
             qt[h, HEAD:, :] = (bias_ref[r].astype(F32) - top).astype(BF16)
@@ -129,23 +145,22 @@
         dos[h * QT:(h + 1) * QT] = (g * col).astype(BF16)
         invs.append(inv)
 
-    def backward(i, carry):
-        _, where = blocks(i)
+    def backward(i, wide):
+        _, where = blocks(i, wide)
         k = jnp.concatenate([kv_ref[t, zq, :, :HEAD] for t, zq in where], axis=0)
-        dv = dot(pbuf[i], dos[...])
+        dv = dot(pbuf[i, :wide * BLK], dos[...])
         dss = []
         for h in range(GROUP):
             cols = slice(h * QT, (h + 1) * QT)
-            dss.append((pbuf[i, :, cols].astype(F32) * (dpbuf[i, :, cols] - stat_d[h, :1])).astype(BF16))
+            dss.append((pbuf[i, :wide * BLK, cols].astype(F32) * (dpbuf[i, :wide * BLK, cols].astype(F32) - stat_d[h, :1])).astype(BF16))
         ds = jnp.concatenate(dss, axis=1)
         dqt[...] += dot_tn(k, ds)
         dk = dot(ds, qs[...])
         for j, (t, zq) in enumerate(where):
             acc[t, zq, :, :HEAD] += dk[j * BLK:(j + 1) * BLK]
             acc[t, zq, :, HEAD:] += dv[j * BLK:(j + 1) * BLK]
-        return carry
-
-    lax.fori_loop(0, steps, backward, 0)
+
+    every(backward)
     for tile in range(NQ):
         @pl.when(r == tile)
         def _():
@@ -179,12 +194,13 @@
             scratch_shapes=[
                 pltpu.VMEM((Z * BLK, 2 * GROUP * HEAD), BF16),
                 pltpu.VMEM((T, Z, BLK, 2 * HEAD), F32),
-                pltpu.VMEM((NI, KT, GROUP * QT), F32),
+                pltpu.VMEM((NI, KT, GROUP * QT), BF16),
                 pltpu.VMEM((NI, KT, GROUP * QT), BF16),
                 pltpu.VMEM((GROUP, 2 * HEAD, QT), BF16),
                 pltpu.VMEM((GROUP, HEAD, QT), BF16),
                 pltpu.VMEM((GROUP * QT, HEAD), BF16),
                 pltpu.VMEM((GROUP * QT, HEAD), BF16),
+                pltpu.VMEM((GROUP, 8, QT), F32),
                 pltpu.VMEM((GROUP, 8, QT), F32),
                 pltpu.VMEM((GROUP, 8, QT), F32),
                 pltpu.VMEM((GROUP, 8, QT), F32),

time: 178 us -> 173 us (0.972); the launches traced: 180 us -> 171 us
  Pallas kernels: 56.7 us -> 47.5 us
  starting transfers between devices: 42.5 us -> 49.1 us
  waiting for transfers between devices: 55.1 us -> 48.5 us
    pallas_call x1, Pallas kernels: 56.7 us -> 47.5 us  [attention(): pl.pallas_call(attn_kernel, grid_spec=pltpu.PrefetchScalarGridSpec(num_sc...]
    ppermute x16, waiting for transfers between devices: 55.1 us -> 48.4 us  [shift(): return lax.ppermute(x, axis, [(i, (i + k) % size) for i in range(size)])]
    ppermute x16, starting transfers between devices: 42.5 us -> 49.1 us  [shift(): return lax.ppermute(x, axis, [(i, (i + k) % size) for i in range(size)])]
where the time goes in v6:
time: 173 us; the launch traced here: 171 us
  starting transfers between devices  49.1 us (28%)
  waiting for transfers between devices  48.5 us (28%)
  Pallas kernels  47.5 us (27%)
  between operations  14.3 us (8%)
  other arithmetic  8.03 us (5%)
  local copies, waits for them, and re-layouts  3.33 us (2%)
    ppermute x16, starting transfers between devices, shift(): return lax.ppermute(x, axis, [(i, (i + k) % size) for i in range(size)])  49.1 us
    ppermute x16, waiting for transfers between devices, shift(): return lax.ppermute(x, axis, [(i, (i + k) % size) for i in range(size)])  48.4 us
    pallas_call x1, Pallas kernels, attention(): pl.pallas_call(attn_kernel, grid_spec=pltpu.PrefetchScalarGridSpec(num_sc...  47.5 us
  transfers between devices with their start and end apart: 17, of which 11 were waited for; matrix products, arithmetic and copies ran while one was open for 4% of the time, Pallas kernels for 0%

profile of v6, /device:TPU:2, one launch (start us, length us, event | category | flops | bytes accessed | tf_op | source)
XLA Modules:
  0.0 170.9 jit_solution(4060090227802723523)
XLA Ops:
  7.3 1.1 constant_dynamic-slice_fusion.9
  8.4 6.4 %collective-permute-start.2 = (bf16[192,256]{1,0:T(8,128)(2,1)S(1)}, bf16[192,256]{1,0:T(8,128)(2,1)S(1)}, u32[]{:S(2)}, u32[]{:S(2)}) collective-permute-start(bf16[192,256]{1,0:T(8,128)(2,1)S(1)} %pad_maximum_fusion.13), channel_id=1, source_target_pairs={{0,192},{64,0},{128,64},{192,128},{1,193},{65,1},{129,65},{193,129... | collective-permute-start | bytes 294920 | tf_op jit(solution)/shard_map/ppermute | solution.py:252
  14.8 1.0 collective-permute-start.1
  15.9 3.0 %collective-permute-start = (bf16[192,256]{1,0:T(8,128)(2,1)S(1)}, bf16[192,256]{1,0:T(8,128)(2,1)S(1)}, u32[]{:S(2)}, u32[]{:S(2)}) collective-permute-start(bf16[192,256]{1,0:T(8,128)(2,1)S(1)} %pad_maximum_fusion.11), channel_id=1, source_target_pairs={{0,64},{64,128},{128,192},{192,0},{1,65},{65,129},{129,193},{193,1... | collective-permute-start | bytes 294920 | tf_op jit(solution)/shard_map/ppermute | solution.py:252
  18.8 0.8 reshape.61
  21.6 2.5 %fusion.hot_ref = bf16[33,192,128]{2,1,0:T(8,128)(2,1)} fusion(s32[33,192]{1,0:T(8,128)S(1)} %concatenate.44), kind=kLoop, calls=%fused_computation.1 | loop fusion | flops 1622016 | bytes 1647360 | tf_op jit(solution)/shard_map/convert_element_type | solution.py:227
  24.5 1.9 %collective-permute-done.1 = bf16[192,256]{1,0:T(8,128)(2,1)S(1)} collective-permute-done((bf16[192,256]{1,0:T(8,128)(2,1)S(1)}, bf16[192,256]{1,0:T(8,128)(2,1)S(1)}, u32[]{:S(2)}, u32[]{:S(2)}) %collective-permute-start.1) | collective-permute-done | bytes 98336 | tf_op jit(solution)/shard_map/ppermute | solution.py:252
  26.4 0.8 pad_maximum_fusion.2
  27.2 0.9 collective-permute-start.3
  28.1 4.1 %collective-permute-start.4 = (bf16[192,768]{1,0:T(8,128)(2,1)S(1)}, bf16[192,768]{1,0:T(8,128)(2,1)S(1)}, u32[]{:S(2)}, u32[]{:S(2)}) collective-permute-start(bf16[192,768]{1,0:T(8,128)(2,1)S(1)} %pad_maximum_fusion.6), channel_id=1, source_target_pairs={{0,128},{64,192},{128,0},{192,64},{1,129},{65,193},{129,1},{193,65... | collective-permute-start | bytes 884744 | tf_op jit(solution)/shard_map/ppermute | solution.py:252
  32.1 4.0 %collective-permute-start.5 = (bf16[192,768]{1,0:T(8,128)(2,1)S(1)}, bf16[192,768]{1,0:T(8,128)(2,1)S(1)}, u32[]{:S(2)}, u32[]{:S(2)}) collective-permute-start(bf16[192,768]{1,0:T(8,128)(2,1)S(1)} %pad_maximum_fusion.7), channel_id=1, source_target_pairs={{0,192},{64,0},{128,64},{192,128},{1,193},{65,1},{129,65},{193,129... | collective-permute-start | bytes 884744 | tf_op jit(solution)/shard_map/ppermute | solution.py:252
  36.3 4.6 %collective-permute-done.3.qd1 = bf16[192,768]{1,0:T(8,128)(2,1)S(1)} collective-permute-done((bf16[192,768]{1,0:T(8,128)(2,1)S(1)}, bf16[192,768]{1,0:T(8,128)(2,1)S(1)}, u32[]{:S(2)}, u32[]{:S(2)}) %collective-permute-start.3) | collective-permute-done | bytes 294944 | tf_op jit(solution)/shard_map/ppermute | solution.py:252
  40.9 6.2 %collective-permute-done.4.qd2 = bf16[192,768]{1,0:T(8,128)(2,1)S(1)} collective-permute-done((bf16[192,768]{1,0:T(8,128)(2,1)S(1)}, bf16[192,768]{1,0:T(8,128)(2,1)S(1)}, u32[]{:S(2)}, u32[]{:S(2)}) %collective-permute-start.4) | collective-permute-done | bytes 294944 | tf_op jit(solution)/shard_map/ppermute | solution.py:252
  47.0 11.6 %collective-permute-done.5.qd3 = bf16[192,768]{1,0:T(8,128)(2,1)S(1)} collective-permute-done((bf16[192,768]{1,0:T(8,128)(2,1)S(1)}, bf16[192,768]{1,0:T(8,128)(2,1)S(1)}, u32[]{:S(2)}, u32[]{:S(2)}) %collective-permute-start.5) | collective-permute-done | bytes 294944 | tf_op jit(solution)/shard_map/ppermute | solution.py:252
  58.6 47.5 %shard_map.85 = (bf16[4,192,384]{2,1,0:T(8,128)(2,1)S(1)}, bf16[4,4,192,256]{3,2,1,0:T(8,128)(2,1)S(1)}, bf16[4,4,192,256]{3,2,1,0:T(8,128)(2,1)S(1)}) custom-call(s32[96]{0:T(128)S(1)} %add.169.lists, s32[3]{0:T(128)S(1)} %convert_reduce_fusion.1.counts, s32[3]{0:T(128)S(1)} %pad_add_fusion.spot, bf16[192,768]{1,0:T(8,128)(2,1)S(1)} %pad_maximum_fusion.4.qd0, ...), custom_call_target="tpu_custom_call" | custom-call | tf_op jit(solution)/shard_map/pallas_call | solution.py:187
  106.2 3.4 %collective-permute-done.6 = bf16[4,4,192,256]{3,2,1,0:T(8,128)(2,1)S(1)} collective-permute-done((bf16[4,4,192,256]{3,2,1,0:T(8,128)(2,1)S(1)}, bf16[4,4,192,256]{3,2,1,0:T(8,128)(2,1)S(1)}, u32[]{:S(2)}, u32[]{:S(2)}) %collective-permute-start.6) | collective-permute-done | bytes 1572896 | tf_op jit(solution)/shard_map/ppermute | solution.py:252
  110.1 4.8 %collective-permute-start.7 = (bf16[4,192,256]{2,1,0:T(8,128)(2,1)S(1)}, bf16[4,192,256]{2,1,0:T(8,128)(2,1)S(1)}, u32[]{:S(2)}, u32[]{:S(2)}) collective-permute-start(bf16[4,192,256]{2,1,0:T(8,128)(2,1)S(1)} %get-tuple-element.51), channel_id=1, source_target_pairs={{0,16},{16,32},{32,48},{48,0},{1,17},{17,33},{33,49},{49,1},{2,18}... | collective-permute-start | bytes 1179656 | tf_op jit(solution)/shard_map/ppermute | solution.py:252
  114.9 11.0 %collective-permute-start.8 = (bf16[4,192,256]{2,1,0:T(8,128)(2,1)S(1)}, bf16[4,192,256]{2,1,0:T(8,128)(2,1)S(1)}, u32[]{:S(2)}, u32[]{:S(2)}) collective-permute-start(bf16[4,192,256]{2,1,0:T(8,128)(2,1)S(1)} %get-tuple-element.50), channel_id=1, source_target_pairs={{0,32},{16,48},{32,0},{48,16},{1,33},{17,49},{33,1},{49,17},{2,34}... | collective-permute-start | bytes 1179656 | tf_op jit(solution)/shard_map/ppermute | solution.py:252
  125.8 0.7 slice_bitcast_fusion
  126.6 4.1 %collective-permute-start.10 = (bf16[192,384]{1,0:T(8,128)(2,1)S(1)}, bf16[192,384]{1,0:T(8,128)(2,1)S(1)}, u32[]{:S(2)}, u32[]{:S(2)}) collective-permute-start(bf16[192,384]{1,0:T(8,128)(2,1)S(1)} %get-tuple-element.59), channel_id=1, source_target_pairs={{0,192},{64,0},{128,64},{192,128},{1,193},{65,1},{129,65},{193,129... | collective-permute-start | bytes 442376 | tf_op jit(solution)/shard_map/ppermute | solution.py:252
  130.7 2.0 %collective-permute-start.11 = (bf16[192,384]{1,0:T(8,128)(2,1)}, bf16[192,384]{1,0:T(8,128)(2,1)S(1)}, u32[]{:S(2)}, u32[]{:S(2)}) collective-permute-start(bf16[192,384]{1,0:T(8,128)(2,1)} %get-tuple-element.58), channel_id=1, source_target_pairs={{0,128},{64,192},{128,0},{192,64},{1,129},{65,193},{129,1},{193,65... | collective-permute-start | bytes 442376 | tf_op jit(solution)/shard_map/ppermute | solution.py:252
  132.7 6.3 %collective-permute-done.10 = bf16[192,384]{1,0:T(8,128)(2,1)S(1)} collective-permute-done((bf16[192,384]{1,0:T(8,128)(2,1)S(1)}, bf16[192,384]{1,0:T(8,128)(2,1)S(1)}, u32[]{:S(2)}, u32[]{:S(2)}) %collective-permute-start.10) | collective-permute-done | bytes 147488 | tf_op jit(solution)/shard_map/ppermute | solution.py:252
  139.0 3.2 %collective-permute-start.12 = (bf16[192,384]{1,0:T(8,128)(2,1)S(1)}, bf16[192,384]{1,0:T(8,128)(2,1)S(1)}, u32[]{:S(2)}, u32[]{:S(2)}) collective-permute-start(bf16[192,384]{1,0:T(8,128)(2,1)S(1)} %get-tuple-element.57), channel_id=1, source_target_pairs={{0,64},{64,128},{128,192},{192,0},{1,65},{65,129},{129,193},{193,1... | collective-permute-start | bytes 442376 | tf_op jit(solution)/shard_map/ppermute | solution.py:252
  142.2 2.9 %collective-permute-done.11 = bf16[192,384]{1,0:T(8,128)(2,1)S(1)} collective-permute-done((bf16[192,384]{1,0:T(8,128)(2,1)}, bf16[192,384]{1,0:T(8,128)(2,1)S(1)}, u32[]{:S(2)}, u32[]{:S(2)}) %collective-permute-start.11) | collective-permute-done | bytes 147488 | tf_op jit(solution)/shard_map/ppermute | solution.py:252
  145.1 5.1 %collective-permute-done.12 = bf16[192,384]{1,0:T(8,128)(2,1)S(1)} collective-permute-done((bf16[192,384]{1,0:T(8,128)(2,1)S(1)}, bf16[192,384]{1,0:T(8,128)(2,1)S(1)}, u32[]{:S(2)}, u32[]{:S(2)}) %collective-permute-start.12) | collective-permute-done | bytes 147488 | tf_op jit(solution)/shard_map/ppermute | solution.py:252
  150.4 2.1 %collective-permute-start.13 = (bf16[192,256]{1,0:T(8,128)(2,1)S(1)}, bf16[192,256]{1,0:T(8,128)(2,1)S(1)}, u32[]{:S(2)}, u32[]{:S(2)}) collective-permute-start(bf16[192,256]{1,0:T(8,128)(2,1)S(1)} %get-tuple-element.76), channel_id=1, source_target_pairs={{0,192},{64,0},{128,64},{192,128},{1,193},{65,1},{129,65},{193,129... | collective-permute-start | bytes 294920 | tf_op jit(solution)/shard_map/ppermute | solution.py:252
  152.6 1.8 %collective-permute-start.14 = (bf16[192,256]{1,0:T(8,128)(2,1)S(1)}, bf16[192,256]{1,0:T(8,128)(2,1)S(1)}, u32[]{:S(2)}, u32[]{:S(2)}) collective-permute-start(bf16[192,256]{1,0:T(8,128)(2,1)S(1)} %get-tuple-element.75), channel_id=1, source_target_pairs={{0,128},{64,192},{128,0},{192,64},{1,129},{65,193},{129,1},{193,65... | collective-permute-start | bytes 294920 | tf_op jit(solution)/shard_map/ppermute | solution.py:252
  155.2 0.9 pad_maximum_fusion.1
  156.2 5.4 %collective-permute-done.14 = bf16[192,256]{1,0:T(8,128)(2,1)S(1)} collective-permute-done((bf16[192,256]{1,0:T(8,128)(2,1)S(1)}, bf16[192,256]{1,0:T(8,128)(2,1)S(1)}, u32[]{:S(2)}, u32[]{:S(2)}) %collective-permute-start.14) | collective-permute-done | bytes 98336 | tf_op jit(solution)/shard_map/ppermute | solution.py:252
  161.6 0.9 collective-permute-done.15
  162.7 0.7 pad_maximum_fusion.9
  163.4 0.7 pad_maximum_fusion.8
  (58 shorter events, 4.3 us)
Async XLA Ops:
  7.2 12.5 %copy-start.2 = (s32[6144]{0:T(1024)S(1)}, s32[6144]{0:T(1024)}, u32[]{:S(2)}) copy-start(s32[6144]{0:T(1024)} %param.10) | copy-start | bytes 73732
  7.2 13.4 %copy-start.3 = (s32[16,16]{1,0:T(8,128)S(1)}, s32[16,16]{1,0:T(8,128)}, u32[]{:S(2)}) copy-start(s32[16,16]{1,0:T(8,128)} %param.11) | copy-start | bytes 3076
  7.2 51.4 %all-gather.3.cloned.1.call-start = ((), (), s32[]{:S(2)}) async-start(), calls=%async_computation | async-start | bytes 3538944 | tf_op jit(solution)/shard_map/all_gather | solution.py:270
  7.3 16.8 %copy-start = (bf16[192,1536]{1,0:T(8,128)(2,1)S(1)}, bf16[192,1536]{1,0:T(8,128)(2,1)}, u32[]{:S(2)}) copy-start(bf16[192,1536]{1,0:T(8,128)(2,1)} %param.9) | copy-start | bytes 1769476
  7.3 16.8 %copy-start.1 = (bf16[192,1536]{1,0:T(8,128)(2,1)S(1)}, bf16[192,1536]{1,0:T(8,128)(2,1)}, u32[]{:S(2)}) copy-start(bf16[192,1536]{1,0:T(8,128)(2,1)} %param.6) | copy-start | bytes 1769476
  8.4 16.0 %collective-permute-start.2 = (bf16[192,256]{1,0:T(8,128)(2,1)S(1)}, bf16[192,256]{1,0:T(8,128)(2,1)S(1)}, u32[]{:S(2)}, u32[]{:S(2)}) collective-permute-start(bf16[192,256]{1,0:T(8,128)(2,1)S(1)} %pad_maximum_fusion.13), channel_id=1, source_target_pairs={{0,192},{64,0},{128,64},{192,128},{1,193},{65,1},{129,65},{193,129... | collective-permute-start | bytes 294920 | tf_op jit(solution)/shard_map/ppermute | solution.py:252
  14.8 11.5 %collective-permute-start.1 = (bf16[192,256]{1,0:T(8,128)(2,1)S(1)}, bf16[192,256]{1,0:T(8,128)(2,1)S(1)}, u32[]{:S(2)}, u32[]{:S(2)}) collective-permute-start(bf16[192,256]{1,0:T(8,128)(2,1)S(1)} %pad_maximum_fusion.12), channel_id=1, source_target_pairs={{0,128},{64,192},{128,0},{192,64},{1,129},{65,193},{129,1},{193,65... | collective-permute-start | bytes 294920 | tf_op jit(solution)/shard_map/ppermute | solution.py:252
  15.9 10.5 %collective-permute-start = (bf16[192,256]{1,0:T(8,128)(2,1)S(1)}, bf16[192,256]{1,0:T(8,128)(2,1)S(1)}, u32[]{:S(2)}, u32[]{:S(2)}) collective-permute-start(bf16[192,256]{1,0:T(8,128)(2,1)S(1)} %pad_maximum_fusion.11), channel_id=1, source_target_pairs={{0,64},{64,128},{128,192},{192,0},{1,65},{65,129},{129,193},{193,1... | collective-permute-start | bytes 294920 | tf_op jit(solution)/shard_map/ppermute | solution.py:252
  27.2 13.7 %collective-permute-start.3 = (bf16[192,768]{1,0:T(8,128)(2,1)S(1)}, bf16[192,768]{1,0:T(8,128)(2,1)S(1)}, u32[]{:S(2)}, u32[]{:S(2)}) collective-permute-start(bf16[192,768]{1,0:T(8,128)(2,1)S(1)} %pad_maximum_fusion.5), channel_id=1, source_target_pairs={{0,64},{64,128},{128,192},{192,0},{1,65},{65,129},{129,193},{193,1... | collective-permute-start | bytes 884744 | tf_op jit(solution)/shard_map/ppermute | solution.py:252
  28.1 18.9 %collective-permute-start.4 = (bf16[192,768]{1,0:T(8,128)(2,1)S(1)}, bf16[192,768]{1,0:T(8,128)(2,1)S(1)}, u32[]{:S(2)}, u32[]{:S(2)}) collective-permute-start(bf16[192,768]{1,0:T(8,128)(2,1)S(1)} %pad_maximum_fusion.6), channel_id=1, source_target_pairs={{0,128},{64,192},{128,0},{192,64},{1,129},{65,193},{129,1},{193,65... | collective-permute-start | bytes 884744 | tf_op jit(solution)/shard_map/ppermute | solution.py:252
  32.1 26.5 %collective-permute-start.5 = (bf16[192,768]{1,0:T(8,128)(2,1)S(1)}, bf16[192,768]{1,0:T(8,128)(2,1)S(1)}, u32[]{:S(2)}, u32[]{:S(2)}) collective-permute-start(bf16[192,768]{1,0:T(8,128)(2,1)S(1)} %pad_maximum_fusion.7), channel_id=1, source_target_pairs={{0,192},{64,0},{128,64},{192,128},{1,193},{65,1},{129,65},{193,129... | collective-permute-start | bytes 884744 | tf_op jit(solution)/shard_map/ppermute | solution.py:252
  106.1 3.5 %collective-permute-start.6 = (bf16[4,4,192,256]{3,2,1,0:T(8,128)(2,1)S(1)}, bf16[4,4,192,256]{3,2,1,0:T(8,128)(2,1)S(1)}, u32[]{:S(2)}, u32[]{:S(2)}) collective-permute-start(bf16[4,4,192,256]{3,2,1,0:T(8,128)(2,1)S(1)} %get-tuple-element.39), channel_id=1, source_target_pairs={{0,8},{8,0},{1,9},{9,1},{2,10},{10,2},{3,11},{11,3},{4,12},{12,4},... | collective-permute-start | bytes 4718600 | tf_op jit(solution)/shard_map/ppermute | solution.py:252
  110.1 40.1 %collective-permute-start.7 = (bf16[4,192,256]{2,1,0:T(8,128)(2,1)S(1)}, bf16[4,192,256]{2,1,0:T(8,128)(2,1)S(1)}, u32[]{:S(2)}, u32[]{:S(2)}) collective-permute-start(bf16[4,192,256]{2,1,0:T(8,128)(2,1)S(1)} %get-tuple-element.51), channel_id=1, source_target_pairs={{0,16},{16,32},{32,48},{48,0},{1,17},{17,33},{33,49},{49,1},{2,18}... | collective-permute-start | bytes 1179656 | tf_op jit(solution)/shard_map/ppermute | solution.py:252
  114.9 35.3 %collective-permute-start.8 = (bf16[4,192,256]{2,1,0:T(8,128)(2,1)S(1)}, bf16[4,192,256]{2,1,0:T(8,128)(2,1)S(1)}, u32[]{:S(2)}, u32[]{:S(2)}) collective-permute-start(bf16[4,192,256]{2,1,0:T(8,128)(2,1)S(1)} %get-tuple-element.50), channel_id=1, source_target_pairs={{0,32},{16,48},{32,0},{48,16},{1,33},{17,49},{33,1},{49,17},{2,34}... | collective-permute-start | bytes 1179656 | tf_op jit(solution)/shard_map/ppermute | solution.py:252
  125.8 24.4 %collective-permute-start.9 = (bf16[4,192,256]{2,1,0:T(8,128)(2,1)S(1)}, bf16[4,192,256]{2,1,0:T(8,128)(2,1)S(1)}, u32[]{:S(2)}, u32[]{:S(2)}) collective-permute-start(bf16[4,192,256]{2,1,0:T(8,128)(2,1)S(1)} %get-tuple-element.49), channel_id=1, source_target_pairs={{0,48},{16,0},{32,16},{48,32},{1,49},{17,1},{33,17},{49,33},{2,50}... | collective-permute-start | bytes 1179656 | tf_op jit(solution)/shard_map/ppermute | solution.py:252
  126.6 12.4 %collective-permute-start.10 = (bf16[192,384]{1,0:T(8,128)(2,1)S(1)}, bf16[192,384]{1,0:T(8,128)(2,1)S(1)}, u32[]{:S(2)}, u32[]{:S(2)}) collective-permute-start(bf16[192,384]{1,0:T(8,128)(2,1)S(1)} %get-tuple-element.59), channel_id=1, source_target_pairs={{0,192},{64,0},{128,64},{192,128},{1,193},{65,1},{129,65},{193,129... | collective-permute-start | bytes 442376 | tf_op jit(solution)/shard_map/ppermute | solution.py:252
  130.7 14.4 %collective-permute-start.11 = (bf16[192,384]{1,0:T(8,128)(2,1)}, bf16[192,384]{1,0:T(8,128)(2,1)S(1)}, u32[]{:S(2)}, u32[]{:S(2)}) collective-permute-start(bf16[192,384]{1,0:T(8,128)(2,1)} %get-tuple-element.58), channel_id=1, source_target_pairs={{0,128},{64,192},{128,0},{192,64},{1,129},{65,193},{129,1},{193,65... | collective-permute-start | bytes 442376 | tf_op jit(solution)/shard_map/ppermute | solution.py:252
  139.0 11.2 %collective-permute-start.12 = (bf16[192,384]{1,0:T(8,128)(2,1)S(1)}, bf16[192,384]{1,0:T(8,128)(2,1)S(1)}, u32[]{:S(2)}, u32[]{:S(2)}) collective-permute-start(bf16[192,384]{1,0:T(8,128)(2,1)S(1)} %get-tuple-element.57), channel_id=1, source_target_pairs={{0,64},{64,128},{128,192},{192,0},{1,65},{65,129},{129,193},{193,1... | collective-permute-start | bytes 442376 | tf_op jit(solution)/shard_map/ppermute | solution.py:252
  150.4 5.7 %collective-permute-start.13 = (bf16[192,256]{1,0:T(8,128)(2,1)S(1)}, bf16[192,256]{1,0:T(8,128)(2,1)S(1)}, u32[]{:S(2)}, u32[]{:S(2)}) collective-permute-start(bf16[192,256]{1,0:T(8,128)(2,1)S(1)} %get-tuple-element.76), channel_id=1, source_target_pairs={{0,192},{64,0},{128,64},{192,128},{1,193},{65,1},{129,65},{193,129... | collective-permute-start | bytes 294920 | tf_op jit(solution)/shard_map/ppermute | solution.py:252
  152.6 9.1 %collective-permute-start.14 = (bf16[192,256]{1,0:T(8,128)(2,1)S(1)}, bf16[192,256]{1,0:T(8,128)(2,1)S(1)}, u32[]{:S(2)}, u32[]{:S(2)}) collective-permute-start(bf16[192,256]{1,0:T(8,128)(2,1)S(1)} %get-tuple-element.75), channel_id=1, source_target_pairs={{0,128},{64,192},{128,0},{192,64},{1,129},{65,193},{129,1},{193,65... | collective-permute-start | bytes 294920 | tf_op jit(solution)/shard_map/ppermute | solution.py:252
  154.4 8.1 %collective-permute-start.15 = (bf16[192,256]{1,0:T(8,128)(2,1)S(1)}, bf16[192,256]{1,0:T(8,128)(2,1)S(1)}, u32[]{:S(2)}, u32[]{:S(2)}) collective-permute-start(bf16[192,256]{1,0:T(8,128)(2,1)S(1)} %get-tuple-element.74), channel_id=1, source_target_pairs={{0,64},{64,128},{128,192},{192,0},{1,65},{65,129},{129,193},{193,1... | collective-permute-start | bytes 294920 | tf_op jit(solution)/shard_map/ppermute | solution.py:252
Sparse Core Ops, SparseCore 0:
  27.3 30.8 all-gather.2
